TPU v7x, 32 devices: a whole 2x2x4 slice. The times are simulated.
32 devices in a mesh: out: 4 (over x, core), in: 8 (over z, y).
Axes of the slice: x: 2, y: 2, z: 4, core: 2. Of those that a mesh axis runs over, the one named last changes fastest.
Arguments:
- cotangent: bfloat16 [2048, 16384], P('in', 'out'), may hold values from -25.588427 to 25.588427
- activations: bfloat16 [2048, 16384], P('out', 'in'), may hold values from -1158 to 1158
- basis_out: bfloat16 [16384, 1024], P('out'), may hold values from -1 to 1, as said below
- basis_in: bfloat16 [16384, 1024], P('in'), may hold values from -1 to 1, as said below
Outputs:
- projected: float32 [16384, 16384], P('out', 'in')
Inputs may be any that keep to these rules, and one draw needn't show every extreme that they name: The columns of basis_out are orthonormal before rounding to bfloat16. The columns of basis_in are orthonormal before rounding to bfloat16.
All inputs are finite; a program needn't handle non-finite values.
Results may differ from a plain program's by a relative error of at most 0.018.
Values may be sent and summed in bfloat16 or wider, within the bound.
No kernel may reach another device: no remote copies, remote signals or barrier semaphores. Data moves between devices by JAX's collectives and lax.ppermute only.
A program may use at most 128 MiB of HBM per device.

v0:
```python
import jax
import jax.numpy as jnp
from jax import lax
from jax.sharding import PartitionSpec as P


def body(cotangent, activations, basis_out, basis_in):
    gathered_rows = lax.all_gather(activations, "out", axis=0, tiled=True)
    gradient = lax.dot_general(
        lax.all_gather(cotangent, "in", axis=0, tiled=True),
        gathered_rows,
        (((0,), (0,)), ((), ())),
        preferred_element_type=jnp.float32,
    )
    gradient_low = gradient.astype(jnp.bfloat16)
    row_share = lax.psum_scatter(
        lax.dot_general(
            basis_in, gradient_low, (((0,), (1,)), ((), ())), preferred_element_type=jnp.float32
        ).astype(jnp.bfloat16),
        "in",
        scatter_dimension=0,
        tiled=True,
    )
    core_part = jnp.dot(row_share, basis_out, preferred_element_type=jnp.float32)
    core_share = lax.psum(core_part.astype(jnp.bfloat16), "out")
    expansion_share = lax.dot_general(
        core_share, basis_out, (((1,), (1,)), ((), ())), preferred_element_type=jnp.float32
    ).astype(jnp.bfloat16)
    expansion_all = lax.all_gather(expansion_share, "in", axis=0, tiled=True)
    removal = lax.dot_general(
        expansion_all, basis_in, (((0,), (1,)), ((), ())), preferred_element_type=jnp.float32
    )
    return gradient - removal


def solution(mesh):
    placed = (P("in", "out"), P("out", "in"), P("out", None), P("in", None))
    return jax.shard_map(
        body, mesh=mesh, in_specs=placed, out_specs=P("out", "in"), check_vma=False
    )
```

profile of v0, /device:TPU:0, one launch (start us, length us, event | category | flops | bytes accessed | tf_op | source)
XLA Modules:
  0.0 735.2 jit_solution(3145005624222085367)
XLA Ops:
  6.5 0.0 all-gather.6.cloned.1.call-start
  6.5 0.7 all-gather.6.cloned.1.call-update
  7.3 0.0 all-gather.4.cloned.1.call-start
  7.3 0.7 all-gather.4.cloned.1.call-update
  8.0 0.0 reduce-scatter.4.cloned.1.call-start
  8.1 61.9 %all-gather.6.cloned.1.call-done = bf16[2048,2048]{1,0:T(8,128)(2,1)} async-done(((bf16[512,2048]{1,0:T(8,128)(2,1)}), bf16[2048,2048]{1,0:T(8,128)(2,1)}) %all-gather.6.cloned.1.call-update) | async-done | bytes 8388624 | tf_op jit(solution)/shard_map/all_gather | solution.py:8
  69.9 229.8 %all-gather.4.cloned.1.call-done = bf16[2048,4096]{1,0:T(8,128)(2,1)} async-done(((bf16[256,4096]{1,0:T(8,128)(2,1)}), bf16[2048,4096]{1,0:T(8,128)(2,1)}) %all-gather.4.cloned.1.call-update) | async-done | bytes 16777232 | tf_op jit(solution)/shard_map/all_gather | solution.py:10
  299.7 0.0 copy-start
  299.7 44.0 %fusion.4 = f32[4096,2048]{1,0:T(8,128)} fusion(bf16[2048,4096]{1,0:T(8,128)(2,1)} %all-gather.4.cloned.1.call-done, bf16[2048,2048]{1,0:T(8,128)(2,1)} %all-gather.6.cloned.1.call-done), kind=kOutput, calls=%fused_computation.6 | convolution fusion | flops 34359738368 | bytes 58720256 | tf_op jit(solution)/shard_map/dot_general | solution.py:9
  343.7 0.0 copy-done
  343.7 24.0 %convert_bitcast_fusion = bf16[1024,4096]{0,1:T(8,128)(2,1)} fusion(bf16[2048,1024]{1,0:T(8,128)(2,1)S(1)} %copy-done, f32[4096,2048]{1,0:T(8,128)} %fusion.4), kind=kOutput, calls=%fused_computation.3 | convolution fusion | flops 17192452096 | bytes 46137344 | tf_op jit(solution)/shard_map/dot_general | solution.py:17
  367.7 11.3 %copy.5 = bf16[1024,4096]{1,0:T(8,128)(2,1)} copy(bf16[1024,4096]{0,1:T(8,128)(2,1)} %convert_bitcast_fusion) | data formatting | bytes 16777216
  379.1 0.0 reduce-scatter.4.cloned.1.call-update
  379.1 0.0 all-reduce.2.cloned.1.call-start
  379.1 147.3 %reduce-scatter.4.cloned.1.call-done = bf16[128,4096]{1,0:T(8,128)(2,1)} async-done(((bf16[1024,4096]{1,0:T(8,128)(2,1)}), bf16[128,4096]{1,0:T(8,128)(2,1)}) %reduce-scatter.4.cloned.1.call-update) | async-done | bytes 1048592
  526.4 5.7 convolution_convert_fusion.1
  532.1 0.0 all-reduce.2.cloned.1.call-update
  532.1 0.0 all-gather.8.cloned.1.call-start
  532.2 31.1 %all-reduce.2.cloned.1.call-done = bf16[128,1024]{1,0:T(8,128)(2,1)} async-done(((bf16[128,1024]{1,0:T(8,128)(2,1)}), bf16[128,1024]{1,0:T(8,128)(2,1)}) %all-reduce.2.cloned.1.call-update) | async-done | bytes 262160 | tf_op jit(solution)/shard_map/psum | solution.py:25
  563.3 7.4 %convolution_convert_fusion = bf16[128,4096]{1,0:T(8,128)(2,1)} fusion(bf16[128,1024]{1,0:T(8,128)(2,1)} %all-reduce.2.cloned.1.call-done, bf16[4096,1024]{1,0:T(8,128)(2,1)} %param.6), kind=kOutput, calls=%fused_computation.4 | convolution fusion | flops 1074266112 | bytes 9699328 | tf_op jit(solution)/shard_map/dot_general | solution.py:26
  570.7 0.0 all-gather.8.cloned.1.call-update
  570.7 125.1 %all-gather.8.cloned.1.call-done = bf16[1024,4096]{1,0:T(8,128)(2,1)} async-done(((bf16[128,4096]{1,0:T(8,128)(2,1)}), bf16[1024,4096]{1,0:T(8,128)(2,1)}) %all-gather.8.cloned.1.call-update) | async-done | bytes 8388624 | tf_op jit(solution)/shard_map/all_gather | solution.py:29
  695.8 32.9 %convolution_subtract_fusion = f32[4096,2048]{1,0:T(8,128)} fusion(f32[4096,2048]{1,0:T(8,128)} %fusion.4, bf16[1024,4096]{1,0:T(8,128)(2,1)} %all-gather.8.cloned.1.call-done, bf16[2048,1024]{1,0:T(8,128)(2,1)} %param.7), kind=kOutput, calls=%fused_computation | convolution fusion | flops 17188257792 | bytes 79691776 | tf_op jit(solution)/shard_map/dot_general | solution.py:30
Async XLA Ops:
  6.5 63.4 %all-gather.6.cloned.1.call-start = ((), (), s32[]{:S(2)}) async-start(), calls=%async_computation.2 | async-start | bytes 10485760 | tf_op jit(solution)/shard_map/all_gather | solution.py:8
  7.3 292.5 %all-gather.4.cloned.1.call-start = ((), (), s32[]{:S(2)}) async-start(), calls=%async_computation.1 | async-start | bytes 18874368 | tf_op jit(solution)/shard_map/all_gather | solution.py:10
  8.0 518.4 %reduce-scatter.4.cloned.1.call-start = ((), (), s32[]{:S(2)}) async-start(), calls=%async_computation.5 | async-start | bytes 9437184
  299.7 44.0 %copy-start = (bf16[2048,1024]{1,0:T(8,128)(2,1)S(1)}, bf16[2048,1024]{1,0:T(8,128)(2,1)}, u32[]{:S(2)}) copy-start(bf16[2048,1024]{1,0:T(8,128)(2,1)} %param.7) | copy-start | bytes 12582916
  379.1 184.2 %all-reduce.2.cloned.1.call-start = ((), (), s32[]{:S(2)}) async-start(), calls=%async_computation.3 | async-start | bytes 524288 | tf_op jit(solution)/shard_map/psum | solution.py:25
  532.1 163.7 %all-gather.8.cloned.1.call-start = ((), (), s32[]{:S(2)}) async-start(), calls=%async_computation.4 | async-start | bytes 9437184 | tf_op jit(solution)/shard_map/all_gather | solution.py:29
Sparse Core Ops, SparseCore 0:
  8.9 60.9 all-gather.5
  72.1 227.6 all-gather.3
  379.2 147.1 reduce-scatter.3
  532.3 30.9 all-reduce.1
  570.8 124.9 all-gather.7
where the time goes:
time: 736 us; the launch traced here: 735 us
  waiting for transfers between devices  597 us (81%)
  matrix products  114 us (15%)
  between operations  13.1 us (2%)
  local copies, waits for them, and re-layouts  11.3 us (2%)
    all_gather x1, waiting for transfers between devices, body(): lax.all_gather(cotangent, 'in', axis=0, tiled=True)  230 us
    unnamed x6, waiting for transfers between devices  149 us
    all_gather x1, waiting for transfers between devices, body(): expansion_all = lax.all_gather(expansion_share, 'in', axis=0, tiled=True)  125 us
    all_gather x1, waiting for transfers between devices, body(): gathered_rows = lax.all_gather(activations, 'out', axis=0, tiled=True)  61.9 us
    dot_general x1, matrix products, body(): lax.dot_general(lax.all_gather(cotangent, 'in', axis=0, tiled=True), gath...  44 us
    dot_general x1, matrix products, body(): lax.dot_general(expansion_all, basis_in, (((0,), (1,)), ((), ())), prefer...  32.9 us
    psum x1, waiting for transfers between devices, body(): core_share = lax.psum(core_part.astype(jnp.bfloat16), 'out')  31.1 us
    dot_general x1, matrix products, body(): lax.dot_general(basis_in, gradient_low, (((0,), (1,)), ((), ())), preferr...  24 us
  transfers between devices with their start and end apart: 5, of which 5 were waited for; matrix products, arithmetic and copies ran while one was open for 0% of the time, Pallas kernels for 0%

commit v1 on v0

v1 whole, which is shorter than its diff:
```python
import functools

import jax
import jax.numpy as jnp
from jax import lax
from jax.experimental import pallas as pl
from jax.experimental.pallas import tpu as pltpu
from jax.sharding import PartitionSpec as P

FIRST = (((0,), (0,)), ((), ()))
LAST = (((1,), (1,)), ((), ()))
F32, BF16 = jnp.float32, jnp.bfloat16
LANES = 128
PARTS = (1, 1, 2, 2, 1, 1)
FIRST_EVENTS = ("r0", "r1", "q0", "p0", "r0", "q1", "p1", "r1", "q2", "p2", "r0", "c0", "r1", "c1", "r0", "r2", "c2", "r1", "r3", "c3", "f")
LATER_EVENTS = (
    "m0", "r2", "r3", "m1", "r2", "r3", "r2", "r4", "r3", "r4", "r5", "m2", "r4", "r5", "r4", "m3", "r5", "r5", "m4", "m5",
)


def grid_of(mesh):
    count = mesh.shape["in"]
    places = [d.coords for d in mesh.devices[0]]
    wide = sum(p[2] == places[0][2] for p in places)
    return count // wide, wide


def ring_order(tall, wide):
    if wide < 2 or tall % 2:
        return list(range(tall * wide))
    order = []
    for row in range(tall):
        columns = range(1, wide) if row % 2 == 0 else range(wide - 1, 0, -1)
        order += [row * wide + column for column in columns]
    return order + [row * wide for row in reversed(range(tall))]


def after(x, *others):
    return lax.optimization_barrier((x, *others))[0]


def column_specs(x, block, entries, rows, row_of):
    return [x] * len(entries), [
        pl.BlockSpec((rows, block), functools.partial(lambda e, i, t: (row_of(i), t[e]), e)) for e in entries
    ]


def call(kernel, table, operands, specs, shape, dtype, block, index, steps, flops, total=None):
    aliases = {}
    if total is not None:
        operands, specs = [*operands, total], [*specs, pl.BlockSpec(memory_space=pl.ANY)]
        aliases = {len(operands): 0}
    moved = sum(o.size * o.dtype.itemsize for o in operands[:2])
    return pl.pallas_call(
        kernel,
        out_shape=jax.ShapeDtypeStruct(shape, dtype),
        grid_spec=pltpu.PrefetchScalarGridSpec(
            num_scalar_prefetch=1, grid=(steps,), in_specs=specs, out_specs=pl.BlockSpec(block, index)
        ),
        input_output_aliases=aliases,
        compiler_params=pltpu.CompilerParams(vmem_limit_bytes=40 * 2**20),
        cost_estimate=pl.CostEstimate(flops=flops, bytes_accessed=moved, transcendentals=0),
    )(table, *operands)


def body(tall, wide, cotangent, activations, basis_out, basis_in):
    order = ring_order(tall, wide)
    ring, outs = tall * wide, lax.axis_size("out")
    tokens, height = cotangent.shape
    width, rank = basis_in.shape
    all_tokens = tokens * ring
    mine, here = lax.axis_index("out"), lax.axis_index("in")
    row, column = here // wide, here % wide

    place = jnp.asarray([order.index(i) for i in range(ring)], jnp.int32)[here]
    hops = jnp.asarray([0] + [d for s in range(1, ring // 2) for d in (-s, s)] + [ring // 2], jnp.int32)
    hop = jnp.asarray(order, jnp.int32)[(place + hops + ring) % ring]
    steps = [(a, b) for b in range(wide) for a in range(tall)]
    rows_back = (row - jnp.asarray([a for a, _ in steps], jnp.int32) + tall) % tall
    columns_back = (column - jnp.asarray([b for _, b in steps], jnp.int32) + wide) % wide
    held = rows_back * wide + columns_back
    per = ring // outs
    held_slot = ((held // per) ^ mine) * per + held % per
    in_block = columns_back * tall + rows_back
    out_block = jnp.arange(outs, dtype=jnp.int32) ^ mine
    in_share, out_share = rank // ring, rank // outs

    def turn_rows(x, k):
        return lax.ppermute(x, "in", [(a * wide + b, (a + k) % tall * wide + b) for a in range(tall) for b in range(wide)])

    def turn_columns(x, k):
        return lax.ppermute(x, "in", [(a * wide + b, a * wide + (b + k) % wide) for a in range(tall) for b in range(wide)])

    def swap(x, k):
        return lax.ppermute(x, "out", [(i, i ^ k) for i in range(outs)])

    forward = [(order[k], order[(k + 1) % ring]) for k in range(ring)]
    backward = [(b, a) for a, b in forward]

    def part_of(x, block, size):
        return lax.dynamic_slice_in_dim(x, block * size, size, axis=1)

    def summed(*terms):
        return sum(t.astype(F32) for t in terms).astype(BF16)

    rows = lax.all_gather(activations, "out", axis=0, tiled=True)

    starts = [sum(PARTS[:k]) * height // sum(PARTS) for k in range(len(PARTS))]
    widths = [p * height // sum(PARTS) for p in PARTS]
    shards = [[lax.slice_in_dim(cotangent, s, s + w, axis=1)] for s, w in zip(starts, widths)]
    frontier = []
    state = {}

    def travel(k):
        have = shards[k]
        if len(have) < ring - 1:
            ups, downs = have[max(0, len(have) - 2)], have[-1]
        else:
            half = tokens // 2
            ups, downs = have[-2][:half], have[-1][half:]
        if state.get("loose"):
            state["total"], ups, downs = lax.optimization_barrier((state["total"], ups, downs))
            state["loose"] = False
        if frontier:
            ups, downs = after(ups, *frontier), after(downs, *frontier)
        have += [lax.ppermute(ups, "in", forward), lax.ppermute(downs, "in", backward)]
        return have[-4:-2] if len(have) > 3 else have[:1]

    def multiply(k, total, factor):
        size, tile = widths[k], min(512, width)
        block_rows = sum(PARTS[:k]) // PARTS[k]
        n = ring + 1
        operands = list(shards[k])
        specs = [pl.BlockSpec(x.shape, lambda i, t: (0, 0)) for x in operands]
        operands += [rows] * ring
        specs += [
            pl.BlockSpec((tokens, tile), functools.partial(lambda e, i, t: (t[e], i), e)) for e in range(ring)
        ]
        if out_share % LANES == 0:
            more, more_specs = column_specs(basis_out, out_share, range(ring, ring + outs), size, lambda i: block_rows)
        else:
            fixed = jnp.take(basis_out.reshape(height, outs, out_share), out_block, axis=1).reshape(height, rank)
            more, more_specs = [fixed], [pl.BlockSpec((size, rank), lambda i, t: (block_rows, 0))]
        operands += [*more, factor]
        specs += [*more_specs, pl.BlockSpec((rank, tile), lambda i, t: (0, i))]

        def kernel(table, *refs):
            lefts = [r[...] for r in refs[: n - 2]] + [jnp.concatenate([refs[n - 2][...], refs[n - 1][...]], axis=0)]
            rights = refs[n : n + ring]
            basis = [r[...] for r in refs[n + ring : n + ring + len(more)]]
            basis = basis[0] if len(basis) == 1 else jnp.concatenate(basis, axis=1)
            value = -jnp.dot(basis, refs[n + ring + len(more)][...], preferred_element_type=F32)
            for left, right in zip(lefts, rights):
                value += lax.dot_general(left, right[...], FIRST, preferred_element_type=F32)
            refs[-1][...] = value

        return call(
            kernel, jnp.concatenate([hop, out_block]), operands, specs, (height, width), F32,
            (size, tile), lambda i, t: (block_rows, i), width // tile,
            2 * size * width * (all_tokens + rank), total,
        )


    def coefficients(event):
        if event == "q0":
            part = jnp.dot(activations, basis_in, preferred_element_type=F32).astype(BF16)
            size = tall * in_share
            state["q"] = part_of(part, column, size)
            state["qs"] = [turn_columns(part_of(part, (column + k) % wide, size), k) for k in range(1, wide)]
            return [part]
        if event == "p0":
            x = after(cotangent, *frontier)
            part = jnp.dot(x, basis_out, preferred_element_type=F32).astype(BF16)
            state["p"] = part_of(part, mine, out_share)
            state["ps"] = [swap(part_of(part, mine ^ k, out_share), k) for k in range(1, outs)]
            return [part]
        if event == "q1":
            part = after(summed(state["q"], *state["qs"]), *frontier)
            state["q"] = part_of(part, row, in_share)
            state["qs"] = [turn_rows(part_of(part, (row + k) % tall, in_share), k) for k in range(1, tall)]
            return [part]
        if event == "p1":
            part = after(summed(state["p"], *state["ps"]), *frontier)
            state["ps"] = [part] + [turn_rows(part, k) for k in range(1, tall)]
            return [part]
        if event == "q2":
            part = after(summed(state["q"], *state["qs"]), *frontier)
            state["qs"] = [part] + [swap(part, k) for k in range(1, outs)]
            return [part]
        if event == "p2":
            part = after(jnp.concatenate(state["ps"], axis=0), *frontier)
            state["ps"] = [part] + [turn_columns(part, k) for k in range(1, wide)]
            return [part]
        if event == "c0":
            right = jnp.concatenate(state["qs"], axis=0)
            operands = state["ps"] + [right]
            specs = [pl.BlockSpec(x.shape, lambda i, t: (0, 0)) for x in operands]

            def kernel(table, *refs):
                value = jnp.zeros(refs[-1].shape, F32)
                for e, (a, b) in enumerate(steps):
                    left = refs[b][a * tokens : (a + 1) * tokens, :]
                    at = pl.multiple_of(table[e] * tokens, tokens)
                    value += lax.dot_general(left, refs[wide][pl.ds(at, tokens), :], FIRST, preferred_element_type=F32)
                refs[-1][...] = value.astype(BF16)

            part = call(
                kernel, held_slot, operands, specs, (out_share, in_share), BF16, (out_share, in_share),
                lambda i, t: (0, 0), 1, 2 * all_tokens * out_share * in_share,
            )
            part = after(part, *frontier)
            state["c"] = [part] + [turn_rows(part, k) for k in range(1, tall)]
            return [part]
        if event == "c1":
            part = after(jnp.concatenate(state["c"], axis=1), *frontier)
            state["c"] = [part] + [turn_columns(part, k) for k in range(1, wide)]
            return [part]
        if event == "c2":
            part = after(jnp.concatenate(state["c"], axis=1), *frontier)
            slots = {0: part}
            bit = outs // 2
            slots[bit] = swap(part, bit)
            state["c"] = slots
            for k in (1 << s for s in range(bit.bit_length() - 1)):
                slots[k] = swap(part, k)
            return [part]
        if event == "c3":
            slots = state["c"]
            for k in range(outs):
                if k not in slots:
                    slots[k] = swap(slots[k & ~(k & -k)], k & -k)
            return [slots[outs // 2]]
        cores = [state["c"][k] for k in range(outs)]
        if in_share % LANES == 0:
            more, more_specs = column_specs(basis_in, in_share, range(ring), width, lambda i: 0)
        else:
            more = [jnp.take(basis_in.reshape(width, ring, in_share), in_block, axis=1).reshape(width, rank)]
            more_specs = [pl.BlockSpec((width, rank), lambda i, t: (0, 0))]

        def kernel(table, *refs):
            left = jnp.concatenate([r[...] for r in refs[:outs]], axis=0)
            right = [r[...] for r in refs[outs:-1]]
            right = right[0] if len(right) == 1 else jnp.concatenate(right, axis=1)
            refs[-1][...] = lax.dot_general(left, right, LAST, preferred_element_type=F32).astype(BF16)

        state["f"] = call(
            kernel, in_block, cores + more, [pl.BlockSpec(x.shape, lambda i, t: (0, 0)) for x in cores] + more_specs,
            (rank, width), BF16, (rank, width), lambda i, t: (0, 0), 1, 2 * rank * rank * width,
        )
        return [state["f"]]

    first, later = FIRST_EVENTS, LATER_EVENTS
    if ring // 2 != 4:
        first = [e for e in first if e[0] != "r"]
        later = [e for k in range(len(PARTS)) for e in [f"r{k}"] * (ring // 2) + [f"m{k}"]]
    for event in first:
        frontier = travel(int(event[1])) if event[0] == "r" else coefficients(event)
        if event in ("r0", "r1") and len(shards[int(event[1])]) == 3:
            frontier = []
    state["total"] = None
    for event in later:
        k = int(event[1])
        if event[0] == "r":
            frontier = travel(k)
        else:
            state["total"] = multiply(k, state["total"], state["f"])
            state["loose"] = True
    return state["total"]


def solution(mesh):
    placed = (P("in", "out"), P("out", "in"), P("out", None), P("in", None))
    return jax.shard_map(
        functools.partial(body, *grid_of(mesh)), mesh=mesh, in_specs=placed, out_specs=P("out", "in"), check_vma=False
    )
```

time: 736 us -> 308 us (0.42)
  waiting for transfers between devices: 597 us -> 92.3 us
  matrix products: 114 us -> 13.3 us
  Pallas kernels: 0 us -> 90.3 us
  starting transfers between devices: 0.16 us -> 73 us
  local copies, waits for them, and re-layouts: 11.3 us -> 22.1 us
    all_gather x3 -> x1, waiting for transfers between devices: 417 us -> 0.01 us  [body(): rows = lax.all_gather(activations, 'out', axis=0, tiled=True)]
    unnamed x6 -> x1, waiting for transfers between devices: 149 us -> 0.71 us
    dot_general x5 -> x2, matrix products: 114 us -> 13.3 us  [the longest x1 8.2 us: coefficients(): part = jnp.dot(x, basis_out, preferred_element_type=F32).astype(BF16)]
    ppermute x0 -> x69, waiting for transfers between devices: none -> 91.6 us  [the longest x24 33.8 us: travel(): lax.ppermute(downs, 'in', backward)]
    pallas_call x0 -> x8, Pallas kernels: none -> 90.3 us  [call(): pl.pallas_call(kernel, out_shape=jax.ShapeDtypeStruct(shape, dtype), grid...]
    ppermute x0 -> x69, starting transfers between devices: none -> 73 us  [the longest x24 28.7 us: travel(): lax.ppermute(ups, 'in', forward)]
    psum x1 -> x0, waiting for transfers between devices: 31.1 us -> none  [body(): core_share = lax.psum(core_part.astype(jnp.bfloat16), 'out')]
    unnamed x3 -> x66, local copies, waits for them, and re-layouts: 11.3 us -> 15.4 us
  transfers between devices with their start and end apart: 5 -> 70, of which waited for: 5 -> 28; matrix products, arithmetic and copies ran while one was open for 0% -> 7% of each run, Pallas kernels for 0% -> 26%
where the time goes in v1:
time: 308 us
  waiting for transfers between devices  92.3 us (30%)
  Pallas kernels  90.3 us (29%)
  starting transfers between devices  73 us (24%)
  local copies, waits for them, and re-layouts  22.1 us (7%)
  between operations  13.9 us (5%)
  matrix products  13.3 us (4%)
    pallas_call x8, Pallas kernels, call(): pl.pallas_call(kernel, out_shape=jax.ShapeDtypeStruct(shape, dtype), grid...  90.3 us
    ppermute x24, waiting for transfers between devices, travel(): lax.ppermute(downs, 'in', backward)  33.8 us
    ppermute x24, starting transfers between devices, travel(): lax.ppermute(ups, 'in', forward)  28.7 us
    ppermute x24, waiting for transfers between devices, travel(): lax.ppermute(ups, 'in', forward)  25.5 us
    ppermute x9, starting transfers between devices, turn_rows(): lax.ppermute(x, 'in', [(a * wide + b, (a + k) % tall * wide + b) for a in...  18.2 us
    ppermute x9, waiting for transfers between devices, turn_rows(): lax.ppermute(x, 'in', [(a * wide + b, (a + k) % tall * wide + b) for a in...  15.4 us
    unnamed x66, local copies, waits for them, and re-layouts  15.4 us
    ppermute x24, starting transfers between devices, travel(): lax.ppermute(downs, 'in', backward)  15 us
  transfers between devices with their start and end apart: 70, of which 28 were waited for; matrix products, arithmetic and copies ran while one was open for 7% of the time, Pallas kernels for 26%

profile of v1, /device:TPU:0, one launch (start us, length us, event | category | flops | bytes accessed | tf_op | source)
XLA Modules:
  0.0 307.7 jit_solution(3749006902424789909)
XLA Ops:
  11.6 5.2 %convolution_convert_fusion = bf16[512,1024]{1,0:T(8,128)(2,1)S(1)} fusion(bf16[512,2048]{1,0:T(8,128)(2,1)} %param.10, bf16[2048,1024]{1,0:T(8,128)(2,1)} %refs_11_.1), kind=kOutput, calls=%fused_computation.1 | convolution fusion | flops 2148007936 | bytes 7340032 | tf_op jit(solution)/shard_map/dot_general | solution.py:166
  19.6 8.2 %convolution_convert_fusion.1 = bf16[256,1024]{1,0:T(8,128)(2,1)S(1)} fusion(bf16[256,4096]{1,0:T(8,128)(2,1)} %param.9, bf16[4096,1024]{1,0:T(8,128)(2,1)} %refs_20_.11), kind=kOutput, calls=%fused_computation.2 | convolution fusion | flops 2147745792 | bytes 11010048 | tf_op jit(solution)/shard_map/dot_general | solution.py:173
  38.0 3.6 %collective-permute-start.15 = (bf16[512,128]{1,0:T(8,128)(2,1)S(1)}, bf16[512,128]{1,0:T(8,128)(2,1)S(1)}, u32[]{:S(2)}, u32[]{:S(2)}) collective-permute-start(bf16[512,128]{1,0:T(8,128)(2,1)S(1)} %get-tuple-element.135), channel_id=1, source_target_pairs={{0,6},{1,7},{2,0},{3,1},{4,2},{5,3},{6,4},{7,5},{8,14},{9,15},{10,... | collective-permute-start | bytes 393224 | tf_op jit(solution)/shard_map/ppermute | solution.py:89
  50.9 3.4 %collective-permute-done.14 = bf16[512,128]{1,0:T(8,128)(2,1)S(1)} collective-permute-done((bf16[512,128]{1,0:T(8,128)(2,1)S(1)}, bf16[512,128]{1,0:T(8,128)(2,1)S(1)}, u32[]{:S(2)}, u32[]{:S(2)}) %collective-permute-start.14) | collective-permute-done | bytes 131104 | tf_op jit(solution)/shard_map/ppermute | solution.py:89
  54.3 5.0 %collective-permute-start.10 = (bf16[256,256]{1,0:T(8,128)(2,1)S(1)}, bf16[256,256]{1,0:T(8,128)(2,1)S(1)}, u32[]{:S(2)}, u32[]{:S(2)}) collective-permute-start(bf16[256,256]{1,0:T(8,128)(2,1)S(1)} %add_convert_fusion.2), channel_id=1, source_target_pairs={{0,2},{1,3},{2,4},{3,5},{4,6},{5,7},{6,0},{7,1},{8,10},{9,11},{10,... | collective-permute-start | bytes 393224 | tf_op jit(solution)/shard_map/ppermute | solution.py:89
  62.3 3.3 %collective-permute-done.10 = bf16[256,256]{1,0:T(8,128)(2,1)S(1)} collective-permute-done((bf16[256,256]{1,0:T(8,128)(2,1)S(1)}, bf16[256,256]{1,0:T(8,128)(2,1)S(1)}, u32[]{:S(2)}, u32[]{:S(2)}) %collective-permute-start.10) | collective-permute-done | bytes 131104 | tf_op jit(solution)/shard_map/ppermute | solution.py:89
  71.1 6.8 %collective-permute-done.18 = bf16[512,128]{1,0:T(8,128)(2,1)S(1)} collective-permute-done((bf16[512,128]{1,0:T(8,128)(2,1)S(1)}, bf16[512,128]{1,0:T(8,128)(2,1)S(1)}, u32[]{:S(2)}, u32[]{:S(2)}) %collective-permute-start.18) | collective-permute-done | bytes 131104 | tf_op jit(solution)/shard_map/ppermute | solution.py:95
  81.7 4.6 %collective-permute-done.21.refs_4_ = bf16[256,512]{1,0:T(8,128)(2,1)S(1)} collective-permute-done((bf16[256,512]{1,0:T(8,128)(2,1)S(1)}, bf16[256,512]{1,0:T(8,128)(2,1)S(1)}, u32[]{:S(2)}, u32[]{:S(2)}) %collective-permute-start.21) | collective-permute-done | bytes 262176 | tf_op jit(solution)/shard_map/ppermute | solution.py:126
  97.8 5.9 %collective-permute-done.34.refs_6_ = bf16[256,512]{1,0:T(8,128)(2,1)S(1)} collective-permute-done((bf16[256,512]{1,0:T(8,128)(2,1)S(1)}, bf16[256,512]{1,0:T(8,128)(2,1)S(1)}, u32[]{:S(2)}, u32[]{:S(2)}) %collective-permute-start.34) | collective-permute-done | bytes 262176 | tf_op jit(solution)/shard_map/ppermute | solution.py:126
  103.8 5.6 %collective-permute-done.27 = bf16[256,512]{1,0:T(8,128)(2,1)S(1)} collective-permute-done((bf16[256,512]{1,0:T(8,128)(2,1)S(1)}, bf16[256,512]{1,0:T(8,128)(2,1)S(1)}, u32[]{:S(2)}, u32[]{:S(2)}) %collective-permute-start.27) | collective-permute-done | bytes 262176 | tf_op jit(solution)/shard_map/ppermute | solution.py:92
  113.0 4.3 %collective-permute-done.22.refs_5_ = bf16[256,512]{1,0:T(8,128)(2,1)S(1)} collective-permute-done((bf16[256,512]{1,0:T(8,128)(2,1)S(1)}, bf16[256,512]{1,0:T(8,128)(2,1)S(1)}, u32[]{:S(2)}, u32[]{:S(2)}) %collective-permute-start.22) | collective-permute-done | bytes 262176 | tf_op jit(solution)/shard_map/ppermute | solution.py:126
  117.4 6.0 %collective-permute-done.23.refs_6_ = bf16[256,512]{1,0:T(8,128)(2,1)S(1)} collective-permute-done((bf16[256,512]{1,0:T(8,128)(2,1)S(1)}, bf16[256,512]{1,0:T(8,128)(2,1)S(1)}, u32[]{:S(2)}, u32[]{:S(2)}) %collective-permute-start.23) | collective-permute-done | bytes 262176 | tf_op jit(solution)/shard_map/ppermute | solution.py:126
  129.2 4.2 %collective-permute-done.42.refs_2_ = bf16[256,1024]{1,0:T(8,128)(2,1)} collective-permute-done((bf16[256,1024]{1,0:T(8,128)(2,1)S(1)}, bf16[256,1024]{1,0:T(8,128)(2,1)}, u32[]{:S(2)}, u32[]{:S(2)}) %collective-permute-start.42) | collective-permute-done | bytes 524320 | tf_op jit(solution)/shard_map/ppermute | solution.py:126
  133.4 3.4 %collective-permute-done.41.refs_1_ = bf16[256,1024]{1,0:T(8,128)(2,1)} collective-permute-done((bf16[256,1024]{1,0:T(8,128)(2,1)S(1)}, bf16[256,1024]{1,0:T(8,128)(2,1)}, u32[]{:S(2)}, u32[]{:S(2)}) %collective-permute-start.41) | collective-permute-done | bytes 524320 | tf_op jit(solution)/shard_map/ppermute | solution.py:126
  141.3 6.4 %shard_map.92.refs_21_ = bf16[1024,2048]{1,0:T(8,128)(2,1)S(1)} custom-call(s32[8]{0:T(128)S(1)} %get-tuple-element.125.table, bf16[256,1024]{1,0:T(8,128)(2,1)S(1)} %pad_maximum_fusion.2.refs_0_, bf16[256,1024]{1,0:T(8,128)(2,1)} %collective-permute-done.30.refs_1_, bf16[256,1024]{1,0:T(8,128)(2,1)} %collective-permute-done.31.refs_2_, ...), custom_call_target="tpu_custom_call" | custom-call | flops 4294967296 | bytes 1048576 | tf_op jit(solution)/shard_map/pallas_call | solution.py:54
  160.7 11.3 %shard_map.93.refs_22_ = f32[4096,2048]{1,0:T(8,128)} custom-call(s32[12]{0:T(128)S(1)} %pad_add_fusion.table, bf16[256,512]{1,0:T(8,128)(2,1)S(1)} %get-tuple-element.130.refs_0_, bf16[256,512]{1,0:T(8,128)(2,1)S(1)} %copy-done.10, bf16[256,512]{1,0:T(8,128)(2,1)S(1)} %copy-done.8, bf16[256,512]{1,0:T(8,128)(2,1)S(1)} %copy-done.20, ...), custom_call_target="tpu_custom_call" | custom-call | flops 6442450944 | bytes 524288 | tf_op jit(solution)/shard_map/pallas_call | solution.py:54
  175.0 11.4 %shard_map.94.refs_22_ = f32[4096,2048]{1,0:T(8,128)} custom-call(s32[12]{0:T(128)S(1)} %pad_add_fusion.table, bf16[256,512]{1,0:T(8,128)(2,1)S(1)} %get-tuple-element.131.refs_0_, bf16[256,512]{1,0:T(8,128)(2,1)S(1)} %copy-done.14, bf16[256,512]{1,0:T(8,128)(2,1)S(1)} %copy-done.12, ...), custom_call_target="tpu_custom_call", output_to_operand_aliasing={{}: (23, {})} | custom-call | flops 6442450944 | bytes 524288 | tf_op jit(solution)/shard_map/pallas_call | solution.py:54
  190.5 10.8 %collective-permute-done.44.refs_6_ = bf16[256,1024]{1,0:T(8,128)(2,1)S(1)} collective-permute-done((bf16[256,1024]{1,0:T(8,128)(2,1)S(1)}, bf16[256,1024]{1,0:T(8,128)(2,1)S(1)}, u32[]{:S(2)}, u32[]{:S(2)}) %collective-permute-start.44) | collective-permute-done | bytes 524320 | tf_op jit(solution)/shard_map/ppermute | solution.py:126
  203.8 9.0 %collective-permute-done.50.refs_5_ = bf16[256,1024]{1,0:T(8,128)(2,1)S(1)} collective-permute-done((bf16[256,1024]{1,0:T(8,128)(2,1)S(1)}, bf16[256,1024]{1,0:T(8,128)(2,1)S(1)}, u32[]{:S(2)}, u32[]{:S(2)}) %collective-permute-start.50) | collective-permute-done | bytes 524320 | tf_op jit(solution)/shard_map/ppermute | solution.py:126
  214.6 3.8 %collective-permute-done.45.refs_1_ = bf16[256,512]{1,0:T(8,128)(2,1)S(1)} collective-permute-done((bf16[256,512]{1,0:T(8,128)(2,1)S(1)}, bf16[256,512]{1,0:T(8,128)(2,1)S(1)}, u32[]{:S(2)}, u32[]{:S(2)}) %collective-permute-start.45) | collective-permute-done | bytes 262176 | tf_op jit(solution)/shard_map/ppermute | solution.py:126
  226.6 18.6 %shard_map.95.refs_22_ = f32[4096,2048]{1,0:T(8,128)} custom-call(s32[12]{0:T(128)S(1)} %pad_add_fusion.table, bf16[256,1024]{1,0:T(8,128)(2,1)S(1)} %get-tuple-element.85.refs_0_, bf16[256,1024]{1,0:T(8,128)(2,1)} %collective-permute-done.37.refs_1_, bf16[256,1024]{1,0:T(8,128)(2,1)S(1)} %copy-done.6, ...), custom_call_target="tpu_custom_call", output_to_operand_aliasing={{}: (23, {})} | custom-call | flops 12884901888 | bytes 1048576 | tf_op jit(solution)/shard_map/pallas_call | solution.py:54
  249.4 19.0 %shard_map.96.refs_22_ = f32[4096,2048]{1,0:T(8,128)} custom-call(s32[12]{0:T(128)S(1)} %pad_add_fusion.table, bf16[256,1024]{1,0:T(8,128)(2,1)S(1)} %get-tuple-element.92.refs_0_, bf16[256,1024]{1,0:T(8,128)(2,1)} %collective-permute-done.41.refs_1_, bf16[256,1024]{1,0:T(8,128)(2,1)} %collective-permute-done.42.refs_2_, ...), custom_call_target="tpu_custom_call", output_to_operand_aliasing={{}: (23, {})} | custom-call | flops 12884901888 | bytes 1048576 | tf_op jit(solution)/shard_map/pallas_call | solution.py:54
  278.2 11.3 %shard_map.97.refs_22_ = f32[4096,2048]{1,0:T(8,128)} custom-call(s32[12]{0:T(128)S(1)} %pad_add_fusion.table, bf16[256,512]{1,0:T(8,128)(2,1)S(1)} %get-tuple-element.96.refs_0_, bf16[256,512]{1,0:T(8,128)(2,1)S(1)} %collective-permute-done.45.refs_1_, bf16[256,512]{1,0:T(8,128)(2,1)S(1)} %collective-permute-done.46.refs_2_, ...), custom_call_target="tpu_custom_call", output_to_operand_aliasing={{}: (23, {})} | custom-call | flops 6442450944 | bytes 524288 | tf_op jit(solution)/shard_map/pallas_call | solution.py:54
  289.5 11.3 %shard_map.98 = f32[4096,2048]{1,0:T(8,128)} custom-call(s32[12]{0:T(128)S(1)} %pad_add_fusion.table, bf16[256,512]{1,0:T(8,128)(2,1)S(1)} %get-tuple-element.97.refs_0_, bf16[256,512]{1,0:T(8,128)(2,1)S(1)} %collective-permute-done.47.refs_1_, bf16[256,512]{1,0:T(8,128)(2,1)S(1)} %collective-permute-done.48.refs_2_, ...), custom_call_target="tpu_custom_call", output_to_operand_aliasing={{}: (23, {})} | custom-call | flops 6442450944 | bytes 524288 | tf_op jit(solution)/shard_map/pallas_call | solution.py:54
  (224 shorter events, 111.3 us)
Async XLA Ops:
  6.5 146.3 %all-gather.2.cloned.1.call-start = ((), (), s32[]{:S(2)}) async-start(), calls=%async_computation | async-start | bytes 10485760 | tf_op jit(solution)/shard_map/all_gather | solution.py:106
  8.5 24.5 %collective-permute-start.7 = (bf16[256,512]{1,0:T(8,128)(2,1)S(1)}, bf16[256,512]{1,0:T(8,128)(2,1)S(1)}, u32[]{:S(2)}, u32[]{:S(2)}) collective-permute-start(bf16[256,512]{1,0:T(8,128)(2,1)S(1)} %get-tuple-element.130.refs_0_), channel_id=1, source_target_pairs={{3,1},{5,3},{7,5},{6,7},{4,6},{2,4},{0,2},{1,0},{11,9},{13,11},{15... | collective-permute-start | bytes 786440 | tf_op jit(solution)/shard_map/ppermute | solution.py:126
  11.6 23.1 %collective-permute-start.6 = (bf16[256,512]{1,0:T(8,128)(2,1)S(1)}, bf16[256,512]{1,0:T(8,128)(2,1)S(1)}, u32[]{:S(2)}, u32[]{:S(2)}) collective-permute-start(bf16[256,512]{1,0:T(8,128)(2,1)S(1)} %get-tuple-element.130.refs_0_), channel_id=1, source_target_pairs={{1,3},{3,5},{5,7},{7,6},{6,4},{4,2},{2,0},{0,1},{9,11},{11,13},{13... | collective-permute-start | bytes 786440 | tf_op jit(solution)/shard_map/ppermute | solution.py:126
  33.1 26.3 %collective-permute-start.1 = (bf16[256,512]{1,0:T(8,128)(2,1)S(1)}, bf16[256,512]{1,0:T(8,128)(2,1)S(1)}, u32[]{:S(2)}, u32[]{:S(2)}) collective-permute-start(bf16[256,512]{1,0:T(8,128)(2,1)S(1)} %get-tuple-element.131.refs_0_), channel_id=1, source_target_pairs={{3,1},{5,3},{7,5},{6,7},{4,6},{2,4},{0,2},{1,0},{11,9},{13,11},{15... | collective-permute-start | bytes 786440 | tf_op jit(solution)/shard_map/ppermute | solution.py:126
  34.7 24.7 %collective-permute-start = (bf16[256,512]{1,0:T(8,128)(2,1)S(1)}, bf16[256,512]{1,0:T(8,128)(2,1)S(1)}, u32[]{:S(2)}, u32[]{:S(2)}) collective-permute-start(bf16[256,512]{1,0:T(8,128)(2,1)S(1)} %get-tuple-element.131.refs_0_), channel_id=1, source_target_pairs={{1,3},{3,5},{5,7},{7,6},{6,4},{4,2},{2,0},{0,1},{9,11},{11,13},{13... | collective-permute-start | bytes 786440 | tf_op jit(solution)/shard_map/ppermute | solution.py:126
  67.5 18.7 %collective-permute-start.21 = (bf16[256,512]{1,0:T(8,128)(2,1)S(1)}, bf16[256,512]{1,0:T(8,128)(2,1)S(1)}, u32[]{:S(2)}, u32[]{:S(2)}) collective-permute-start(bf16[256,512]{1,0:T(8,128)(2,1)S(1)} %collective-permute-done.7.refs_2_), channel_id=1, source_target_pairs={{3,1},{5,3},{7,5},{6,7},{4,6},{2,4},{0,2},{1,0},{11,9},{13,11},{15... | collective-permute-start | bytes 786440 | tf_op jit(solution)/shard_map/ppermute | solution.py:126
  103.8 21.6 %collective-permute-start.38 = (bf16[256,1024]{1,0:T(8,128)(2,1)S(1)}, bf16[256,1024]{1,0:T(8,128)(2,1)S(1)}, u32[]{:S(2)}, u32[]{:S(2)}) collective-permute-start(bf16[256,1024]{1,0:T(8,128)(2,1)S(1)} %get-tuple-element.85.refs_0_), channel_id=1, source_target_pairs={{3,1},{5,3},{7,5},{6,7},{4,6},{2,4},{0,2},{1,0},{11,9},{13,11},{15... | collective-permute-start | bytes 1572872 | tf_op jit(solution)/shard_map/ppermute | solution.py:126
  129.2 20.5 %collective-permute-start.35 = (bf16[128,512]{1,0:T(8,128)(2,1)S(1)}, bf16[128,512]{1,0:T(8,128)(2,1)S(1)}, u32[]{:S(2)}, u32[]{:S(2)}) collective-permute-start(bf16[128,512]{1,0:T(8,128)(2,1)S(1)} %slice.76), channel_id=1, source_target_pairs={{1,3},{3,5},{5,7},{7,6},{6,4},{4,2},{2,0},{0,1},{9,11},{11,13},{13... | collective-permute-start | bytes 393224 | tf_op jit(solution)/shard_map/ppermute | solution.py:126
  133.4 18.8 %collective-permute-start.36 = (bf16[128,512]{1,0:T(8,128)(2,1)S(1)}, bf16[128,512]{1,0:T(8,128)(2,1)S(1)}, u32[]{:S(2)}, u32[]{:S(2)}) collective-permute-start(bf16[128,512]{1,0:T(8,128)(2,1)S(1)} %slice.77), channel_id=1, source_target_pairs={{3,1},{5,3},{7,5},{6,7},{4,6},{2,4},{0,2},{1,0},{11,9},{13,11},{15... | collective-permute-start | bytes 393224 | tf_op jit(solution)/shard_map/ppermute | solution.py:126
  136.9 35.4 %collective-permute-start.28 = (bf16[128,512]{1,0:T(8,128)(2,1)}, bf16[128,512]{1,0:T(8,128)(2,1)S(1)}, u32[]{:S(2)}, u32[]{:S(2)}) collective-permute-start(bf16[128,512]{1,0:T(8,128)(2,1)} %slice.74), channel_id=1, source_target_pairs={{1,3},{3,5},{5,7},{7,6},{6,4},{4,2},{2,0},{0,1},{9,11},{11,13},{13... | collective-permute-start | bytes 393224 | tf_op jit(solution)/shard_map/ppermute | solution.py:126
  137.2 36.8 %collective-permute-start.29 = (bf16[128,512]{1,0:T(8,128)(2,1)}, bf16[128,512]{1,0:T(8,128)(2,1)}, u32[]{:S(2)}, u32[]{:S(2)}) collective-permute-start(bf16[128,512]{1,0:T(8,128)(2,1)} %slice.75), channel_id=1, source_target_pairs={{3,1},{5,3},{7,5},{6,7},{4,6},{2,4},{0,2},{1,0},{11,9},{13,11},{15... | collective-permute-start | bytes 393224 | tf_op jit(solution)/shard_map/ppermute | solution.py:126
  138.9 50.0 %collective-permute-start.51 = (bf16[256,1024]{1,0:T(8,128)(2,1)}, bf16[256,1024]{1,0:T(8,128)(2,1)}, u32[]{:S(2)}, u32[]{:S(2)}) collective-permute-start(bf16[256,1024]{1,0:T(8,128)(2,1)} %collective-permute-done.42.refs_2_), channel_id=1, source_target_pairs={{3,1},{5,3},{7,5},{6,7},{4,6},{2,4},{0,2},{1,0},{11,9},{13,11},{15... | collective-permute-start | bytes 1572872 | tf_op jit(solution)/shard_map/ppermute | solution.py:126
  150.4 38.1 %collective-permute-start.49 = (bf16[256,1024]{1,0:T(8,128)(2,1)}, bf16[256,1024]{1,0:T(8,128)(2,1)S(1)}, u32[]{:S(2)}, u32[]{:S(2)}) collective-permute-start(bf16[256,1024]{1,0:T(8,128)(2,1)} %collective-permute-done.41.refs_1_), channel_id=1, source_target_pairs={{1,3},{3,5},{5,7},{7,6},{6,4},{4,2},{2,0},{0,1},{9,11},{11,13},{13... | collective-permute-start | bytes 1572872 | tf_op jit(solution)/shard_map/ppermute | solution.py:126
  188.5 24.3 %collective-permute-start.50 = (bf16[256,1024]{1,0:T(8,128)(2,1)S(1)}, bf16[256,1024]{1,0:T(8,128)(2,1)S(1)}, u32[]{:S(2)}, u32[]{:S(2)}) collective-permute-start(bf16[256,1024]{1,0:T(8,128)(2,1)S(1)} %collective-permute-done.49.refs_3_), channel_id=1, source_target_pairs={{1,3},{3,5},{5,7},{7,6},{6,4},{4,2},{2,0},{0,1},{9,11},{11,13},{13... | collective-permute-start | bytes 1572872 | tf_op jit(solution)/shard_map/ppermute | solution.py:126
  188.9 25.7 %collective-permute-start.52 = (bf16[256,1024]{1,0:T(8,128)(2,1)}, bf16[256,1024]{1,0:T(8,128)(2,1)S(1)}, u32[]{:S(2)}, u32[]{:S(2)}) collective-permute-start(bf16[256,1024]{1,0:T(8,128)(2,1)} %collective-permute-done.51.refs_4_), channel_id=1, source_target_pairs={{3,1},{5,3},{7,5},{6,7},{4,6},{2,4},{0,2},{1,0},{11,9},{13,11},{15... | collective-permute-start | bytes 1572872 | tf_op jit(solution)/shard_map/ppermute | solution.py:126
  203.6 19.9 %collective-permute-start.60 = (bf16[128,1024]{1,0:T(8,128)(2,1)S(1)}, bf16[128,1024]{1,0:T(8,128)(2,1)S(1)}, u32[]{:S(2)}, u32[]{:S(2)}) collective-permute-start(bf16[128,1024]{1,0:T(8,128)(2,1)S(1)} %slice.81), channel_id=1, source_target_pairs={{3,1},{5,3},{7,5},{6,7},{4,6},{2,4},{0,2},{1,0},{11,9},{13,11},{15... | collective-permute-start | bytes 786440 | tf_op jit(solution)/shard_map/ppermute | solution.py:126
  220.2 27.9 %collective-permute-start.57 = (bf16[128,1024]{1,0:T(8,128)(2,1)S(1)}, bf16[128,1024]{1,0:T(8,128)(2,1)S(1)}, u32[]{:S(2)}, u32[]{:S(2)}) collective-permute-start(bf16[128,1024]{1,0:T(8,128)(2,1)S(1)} %slice.78), channel_id=1, source_target_pairs={{1,3},{3,5},{5,7},{7,6},{6,4},{4,2},{2,0},{0,1},{9,11},{11,13},{13... | collective-permute-start | bytes 786440 | tf_op jit(solution)/shard_map/ppermute | solution.py:126
  220.7 28.7 %collective-permute-start.58 = (bf16[128,1024]{1,0:T(8,128)(2,1)S(1)}, bf16[128,1024]{1,0:T(8,128)(2,1)S(1)}, u32[]{:S(2)}, u32[]{:S(2)}) collective-permute-start(bf16[128,1024]{1,0:T(8,128)(2,1)S(1)} %slice.79), channel_id=1, source_target_pairs={{3,1},{5,3},{7,5},{6,7},{4,6},{2,4},{0,2},{1,0},{11,9},{13,11},{15... | collective-permute-start | bytes 786440 | tf_op jit(solution)/shard_map/ppermute | solution.py:126
  223.5 21.8 %collective-permute-start.48 = (bf16[256,512]{1,0:T(8,128)(2,1)S(1)}, bf16[256,512]{1,0:T(8,128)(2,1)S(1)}, u32[]{:S(2)}, u32[]{:S(2)}) collective-permute-start(bf16[256,512]{1,0:T(8,128)(2,1)S(1)} %get-tuple-element.97.refs_0_), channel_id=1, source_target_pairs={{3,1},{5,3},{7,5},{6,7},{4,6},{2,4},{0,2},{1,0},{11,9},{13,11},{15... | collective-permute-start | bytes 786440 | tf_op jit(solution)/shard_map/ppermute | solution.py:126
  223.8 21.5 %collective-permute-start.47 = (bf16[256,512]{1,0:T(8,128)(2,1)S(1)}, bf16[256,512]{1,0:T(8,128)(2,1)S(1)}, u32[]{:S(2)}, u32[]{:S(2)}) collective-permute-start(bf16[256,512]{1,0:T(8,128)(2,1)S(1)} %get-tuple-element.97.refs_0_), channel_id=1, source_target_pairs={{1,3},{3,5},{5,7},{7,6},{6,4},{4,2},{2,0},{0,1},{9,11},{11,13},{13... | collective-permute-start | bytes 786440 | tf_op jit(solution)/shard_map/ppermute | solution.py:126
  245.3 23.1 %collective-permute-start.55 = (bf16[256,512]{1,0:T(8,128)(2,1)S(1)}, bf16[256,512]{1,0:T(8,128)(2,1)S(1)}, u32[]{:S(2)}, u32[]{:S(2)}) collective-permute-start(bf16[256,512]{1,0:T(8,128)(2,1)S(1)} %collective-permute-done.47.refs_1_), channel_id=1, source_target_pairs={{1,3},{3,5},{5,7},{7,6},{6,4},{4,2},{2,0},{0,1},{9,11},{11,13},{13... | collective-permute-start | bytes 786440 | tf_op jit(solution)/shard_map/ppermute | solution.py:126
  247.3 21.1 %collective-permute-start.56 = (bf16[256,512]{1,0:T(8,128)(2,1)S(1)}, bf16[256,512]{1,0:T(8,128)(2,1)S(1)}, u32[]{:S(2)}, u32[]{:S(2)}) collective-permute-start(bf16[256,512]{1,0:T(8,128)(2,1)S(1)} %collective-permute-done.48.refs_2_), channel_id=1, source_target_pairs={{3,1},{5,3},{7,5},{6,7},{4,6},{2,4},{0,2},{1,0},{11,9},{13,11},{15... | collective-permute-start | bytes 786440 | tf_op jit(solution)/shard_map/ppermute | solution.py:126
  247.4 21.0 %collective-permute-start.62 = (bf16[256,512]{1,0:T(8,128)(2,1)S(1)}, bf16[256,512]{1,0:T(8,128)(2,1)S(1)}, u32[]{:S(2)}, u32[]{:S(2)}) collective-permute-start(bf16[256,512]{1,0:T(8,128)(2,1)S(1)} %collective-permute-done.54.refs_4_), channel_id=1, source_target_pairs={{3,1},{5,3},{7,5},{6,7},{4,6},{2,4},{0,2},{1,0},{11,9},{13,11},{15... | collective-permute-start | bytes 786440 | tf_op jit(solution)/shard_map/ppermute | solution.py:126
  248.1 20.3 %collective-permute-start.61 = (bf16[256,512]{1,0:T(8,128)(2,1)S(1)}, bf16[256,512]{1,0:T(8,128)(2,1)S(1)}, u32[]{:S(2)}, u32[]{:S(2)}) collective-permute-start(bf16[256,512]{1,0:T(8,128)(2,1)S(1)} %collective-permute-done.53.refs_3_), channel_id=1, source_target_pairs={{1,3},{3,5},{5,7},{7,6},{6,4},{4,2},{2,0},{0,1},{9,11},{11,13},{13... | collective-permute-start | bytes 786440 | tf_op jit(solution)/shard_map/ppermute | solution.py:126
  (79 other events, 1306.5 us)
Sparse Core Ops, SparseCore 0:
  8.9 72.2 all-gather.1

commit v2 on v0

v2 whole, which is shorter than its diff:
```python
import functools

import jax
import jax.numpy as jnp
import numpy as np
from jax import lax
from jax.experimental import pallas as pl
from jax.experimental.pallas import tpu as pltpu
from jax.sharding import PartitionSpec as P

TOKENS_FIRST = (((0,), (0,)), ((), ()))
LAST_LAST = (((1,), (1,)), ((), ()))
F32, BF16 = jnp.float32, jnp.bfloat16


def ring_order(mesh):
    count = mesh.shape["in"]
    places = [d.coords for d in mesh.devices[0]]
    wide = sum(p[2] == places[0][2] for p in places)
    tall = count // wide
    if wide < 2 or tall % 2:
        return list(range(count))
    order = []
    for row in range(tall):
        columns = range(1, wide) if row % 2 == 0 else range(wide - 1, 0, -1)
        order += [row * wide + column for column in columns]
    return order + [row * wide for row in reversed(range(tall))]


def add_products(offsets, shards, rows_of, low, high, total=None, removal=None, first=0, count=None, tile=512):
    height, width = high, rows_of.shape[1]
    count = height if count is None else count
    tile = min(tile, count)
    tokens = shards[0][0].shape[0]

    def kernel(offsets_ref, *refs):
        n = len(shards)
        value = None
        for left, right in zip(refs[:n], refs[n : 2 * n]):
            term = lax.dot_general(left[...], right[...], TOKENS_FIRST, preferred_element_type=F32)
            value = term if value is None else value + term
        rest = refs[2 * n : -1]
        if removal is not None:
            value = value - jnp.dot(rest[0][...], rest[1][...], preferred_element_type=F32)
        if total is not None:
            value = value + rest[-1][...]
        refs[-1][...] = value.astype(refs[-1].dtype)

    operands = [s[0] for s in shards] + [rows_of] * len(shards)
    specs = [
        pl.BlockSpec((tokens, tile), functools.partial(lambda start, i, offs: (0, start + i), s[1] // tile))
        for s in shards
    ]
    specs += [
        pl.BlockSpec((tokens, width), functools.partial(lambda entry, i, offs: (offs[entry], 0), s[2]))
        for s in shards
    ]
    base = first // tile
    if removal is not None:
        operands += list(removal)
        specs += [
            pl.BlockSpec((tile, removal[0].shape[1]), lambda i, offs: (base + i, 0)),
            pl.BlockSpec(removal[1].shape, lambda i, offs: (0, 0)),
        ]
    aliases = {}
    if total is not None:
        operands.append(total)
        specs.append(pl.BlockSpec((tile, width), lambda i, offs: (base + i, 0)))
        aliases = {len(operands): 0}
    depth = tokens * len(shards) + (removal[0].shape[1] if removal is not None else 0)
    return pl.pallas_call(
        kernel,
        out_shape=jax.ShapeDtypeStruct((height, width), low),
        grid_spec=pltpu.PrefetchScalarGridSpec(
            num_scalar_prefetch=1,
            grid=(count // tile,),
            in_specs=specs,
            out_specs=pl.BlockSpec((tile, width), lambda i, offs: (base + i, 0)),
        ),
        input_output_aliases=aliases,
        compiler_params=pltpu.CompilerParams(vmem_limit_bytes=60 * 2**20),
        cost_estimate=pl.CostEstimate(
            flops=2 * count * width * depth,
            bytes_accessed=count * width * (8 if total is not None else 4) + depth * (count + width) * 2,
            transcendentals=0,
        ),
    )(offsets, *operands)


def stacked(parts):
    rows, width = parts[0].shape
    tile = min(512, width)

    def kernel(*refs):
        for k, r in enumerate(refs[:-1]):
            refs[-1][k * rows : (k + 1) * rows, :] = r[...]

    return pl.pallas_call(
        kernel,
        out_shape=jax.ShapeDtypeStruct((rows * len(parts), width), parts[0].dtype),
        grid=(width // tile,),
        in_specs=[pl.BlockSpec((rows, tile), lambda i: (0, i))] * len(parts),
        out_specs=pl.BlockSpec((rows * len(parts), tile), lambda i: (0, i)),
        compiler_params=pltpu.CompilerParams(vmem_limit_bytes=60 * 2**20),
    )(*parts)


def after(x, *others):
    return lax.optimization_barrier((x, *others))[0]


def body(order, cotangent, activations, basis_out, basis_in):
    ring = len(order)
    outs = lax.axis_size("out")
    forward = [(order[k], order[(k + 1) % ring]) for k in range(ring)]
    backward = [(b, a) for a, b in forward]

    def up(x):
        return lax.ppermute(x, "in", forward)

    def down(x):
        return lax.ppermute(x, "in", backward)

    here, mine = lax.axis_index("in"), lax.axis_index("out")
    per = ring // outs
    hops = [0] + [d for s in range(1, ring // 2) for d in (-s, s)] + [ring // 2]
    lines = [
        [((j // per) ^ o) * per + j % per for j in (order[(order.index(i) + d) % ring] for d in hops)]
        for o in range(outs)
        for i in range(ring)
    ]
    offsets = lax.dynamic_index_in_dim(jnp.asarray(np.asarray(lines, np.int32)), mine * ring + here, keepdims=False)

    height = cotangent.shape[1]
    ups, downs = up(cotangent), down(cotangent)
    shards = [(cotangent, 0, 0), (ups, 0, 1), (downs, 0, 2)]

    share = lax.psum_scatter(
        jnp.dot(cotangent, basis_out, preferred_element_type=F32).astype(BF16),
        "out", scatter_dimension=1, tiled=True,
    )
    coefficients = lax.all_gather(share, "in", axis=0, tiled=True)

    slots = {0: activations}
    bit = outs // 2
    while bit:
        swap = [(i, i ^ bit) for i in range(outs)]
        slots.update({k ^ bit: lax.ppermute(v, "out", swap) for k, v in slots.items()})
        bit //= 2
    rows = stacked([slots[k] for k in range(outs)])

    coefficients = after(coefficients, ups, downs, rows)
    block = coefficients.shape[0] // outs
    coefficients = jnp.concatenate(
        [lax.dynamic_slice_in_dim(coefficients, (mine ^ k) * block, block, axis=0) for k in range(outs)], axis=0
    )
    seen = lax.dot_general(coefficients, rows, TOKENS_FIRST, preferred_element_type=F32).astype(BF16)
    core_part = jnp.dot(seen, basis_in, preferred_element_type=F32).astype(BF16)
    core = lax.psum(core_part, "in")

    total = None
    for step in range(2, ring // 2):
        ups, downs = up(ups), down(downs)
        if step == 2:
            ups, downs, _ = lax.optimization_barrier((ups, downs, core_part))
        shards += [(ups, 0, 2 * step - 1), (downs, 0, 2 * step)]
        if step == 2:
            first = len(shards)
            total = add_products(offsets, shards, rows, F32, height)
    ups, downs, total = lax.optimization_barrier((ups, downs, total))
    half = height // 2
    last = [up(ups[:, :half]), down(downs[:, half:])]
    rest = shards[first:-2] + [(ups, 0, ring - 3), (downs, 0, ring - 2)] if first < len(shards) else []
    core = after(core, ups, downs)
    if rest:
        total = add_products(offsets, rest, rows, F32, height, total, None, 0, half)
    core, total = lax.optimization_barrier((core, total))
    core = lax.all_gather(core, "out", axis=0, tiled=True)
    if rest:
        rest = [(x, half, e) for x, _, e in rest]
        total = add_products(offsets, rest, rows, F32, height, total, None, half, half)
    core, total = lax.optimization_barrier((core, total))
    factor = jnp.dot(core, basis_in.T, preferred_element_type=F32).astype(BF16)
    return remove(offsets, last, rows, total, basis_out, factor, ring - 1)


def remove(offsets, last, rows, total, basis, factor, entry):
    height, width = total.shape
    tokens, half = last[0].shape
    tile = min(256, width)
    rank = factor.shape[0]
    once = pl.Buffered(1)

    def kernel(offsets_ref, left_ref, right_ref, rows_ref, basis_ref, factor_ref, total_ref, out_ref, turned_ref):
        @pl.when(pl.program_id(0) == 0)
        def _():
            turned_ref[:half, :] = left_ref[...].T
            turned_ref[half:, :] = right_ref[...].T

        value = total_ref[...] - jnp.dot(basis_ref[...], factor_ref[...], preferred_element_type=F32)
        out_ref[...] = value + jnp.dot(turned_ref[...], rows_ref[...], preferred_element_type=F32)

    return pl.pallas_call(
        kernel,
        out_shape=jax.ShapeDtypeStruct((height, width), F32),
        grid_spec=pltpu.PrefetchScalarGridSpec(
            num_scalar_prefetch=1,
            grid=(width // tile,),
            in_specs=[
                pl.BlockSpec((tokens, half), lambda i, offs: (0, 0), pipeline_mode=once),
                pl.BlockSpec((tokens, half), lambda i, offs: (0, 0), pipeline_mode=once),
                pl.BlockSpec((tokens, tile), lambda i, offs: (offs[entry], i)),
                pl.BlockSpec((height, rank), lambda i, offs: (0, 0), pipeline_mode=once),
                pl.BlockSpec((rank, tile), lambda i, offs: (0, i)),
                pl.BlockSpec((height, tile), lambda i, offs: (0, i)),
            ],
            out_specs=pl.BlockSpec((height, tile), lambda i, offs: (0, i)),
            scratch_shapes=[pltpu.VMEM((height, tokens), BF16)],
        ),
        input_output_aliases={6: 0},
        compiler_params=pltpu.CompilerParams(vmem_limit_bytes=60 * 2**20),
    )(offsets, last[0], last[1], rows, basis, factor, total)


def solution(mesh):
    placed = (P("in", "out"), P("out", "in"), P("out", None), P("in", None))
    return jax.shard_map(
        functools.partial(body, ring_order(mesh)), mesh=mesh, in_specs=placed, out_specs=P("out", "in"), check_vma=False
    )
```

time: 736 us -> 278 us (0.38)
  waiting for transfers between devices: 597 us -> 116 us
  Pallas kernels: 0 us -> 103 us
  matrix products: 114 us -> 25.3 us
  starting transfers between devices: 0.16 us -> 12.5 us
    all_gather x3 -> x2, waiting for transfers between devices: 417 us -> 40.7 us  [the longest x1 37.3 us: body(): coefficients = lax.all_gather(share, 'in', axis=0, tiled=True)]
    unnamed x6 -> x4, waiting for transfers between devices: 149 us -> 0.07 us
    pallas_call x0 -> x5, Pallas kernels: none -> 103 us  [the longest x3 60 us: add_products(): pl.pallas_call(kernel, out_shape=jax.ShapeDtypeStruct((height, width), lo...]
    dot_general x5 -> x3, matrix products: 114 us -> 25.3 us  [the longest x1 9.34 us: body(): factor = jnp.dot(core, basis_in.T, preferred_element_type=F32).astype(BF16)]
    ppermute x0 -> x11, waiting for transfers between devices: none -> 65.8 us  [the longest x3 41.7 us: body(): lax.ppermute(v, 'out', swap)]
    psum x1, waiting for transfers between devices: 31.1 us -> 9.35 us  [body(): core = lax.psum(core_part, 'in')]
    ppermute x0 -> x11, starting transfers between devices: none -> 12.4 us  [the longest x4 7.6 us: up(): return lax.ppermute(x, 'in', forward)]
    unnamed x3 -> x10, local copies, waits for them, and re-layouts: 11.3 us -> 3.23 us
  transfers between devices with their start and end apart: 5 -> 15, of which waited for: 5 -> 8; matrix products, arithmetic and copies ran while one was open for 0% -> 11% of each run, Pallas kernels for 0% -> 24%
where the time goes in v2:
time: 278 us
  waiting for transfers between devices  116 us (42%)
  Pallas kernels  103 us (37%)
  matrix products  25.3 us (9%)
  between operations  13.2 us (5%)
  starting transfers between devices  12.5 us (4%)
  local copies, waits for them, and re-layouts  8.16 us (3%)
    pallas_call x3, Pallas kernels, add_products(): pl.pallas_call(kernel, out_shape=jax.ShapeDtypeStruct((height, width), lo...  60 us
    ppermute x3, waiting for transfers between devices, body(): lax.ppermute(v, 'out', swap)  41.7 us
    all_gather x1, waiting for transfers between devices, body(): coefficients = lax.all_gather(share, 'in', axis=0, tiled=True)  37.3 us
    pallas_call x1, Pallas kernels, remove(): pl.pallas_call(kernel, out_shape=jax.ShapeDtypeStruct((height, width), F3...  36 us
    ppermute x4, waiting for transfers between devices, up(): return lax.ppermute(x, 'in', forward)  23.9 us
    psum x1, waiting for transfers between devices, body(): core = lax.psum(core_part, 'in')  9.35 us
    dot_general x1, matrix products, body(): factor = jnp.dot(core, basis_in.T, preferred_element_type=F32).astype(BF16)  9.34 us
    dot_general x1, matrix products, body(): core_part = jnp.dot(seen, basis_in, preferred_element_type=F32).astype(BF16)  8.8 us
  transfers between devices with their start and end apart: 15, of which 8 were waited for; matrix products, arithmetic and copies ran while one was open for 11% of the time, Pallas kernels for 24%

profile of v2, /device:TPU:0, one launch (start us, length us, event | category | flops | bytes accessed | tf_op | source)
XLA Modules:
  0.0 278.1 jit_solution(3286579369431448902)
XLA Ops:
  6.5 2.9 %collective-permute-start.5 = (bf16[512,2048]{1,0:T(8,128)(2,1)}, bf16[512,2048]{1,0:T(8,128)(2,1)}, u32[]{:S(2)}, u32[]{:S(2)}) collective-permute-start(bf16[512,2048]{1,0:T(8,128)(2,1)} %refs_0_.2), channel_id=1, source_target_pairs={{0,16},{8,24},{16,0},{24,8},{1,17},{9,25},{17,1},{25,9},{2,18},{10... | collective-permute-start | bytes 6291464 | tf_op jit(solution)/shard_map/ppermute | solution.py:148
  9.5 1.5 collective-permute-start
  11.5 7.1 %convolution_convert_fusion.2 = bf16[256,1024]{1,0:T(8,128)(2,1)} fusion(bf16[256,4096]{1,0:T(8,128)(2,1)} %refs_0_.3, bf16[4096,1024]{1,0:T(8,128)(2,1)} %basis_ref.1), kind=kOutput, calls=%fused_computation.2 | convolution fusion | flops 2147745792 | bytes 11010048 | tf_op jit(solution)/shard_map/dot_general | solution.py:139
  18.8 39.4 %collective-permute-done.5.refs_2_ = bf16[512,2048]{1,0:T(8,128)(2,1)} collective-permute-done((bf16[512,2048]{1,0:T(8,128)(2,1)}, bf16[512,2048]{1,0:T(8,128)(2,1)}, u32[]{:S(2)}, u32[]{:S(2)}) %collective-permute-start.5) | collective-permute-done | bytes 2097184 | tf_op jit(solution)/shard_map/ppermute | solution.py:148
  58.3 1.8 collective-permute-start.1
  60.4 2.3 collective-permute-done.6.refs_3_
  62.7 7.1 %shard_map.55.refs_5_.refs_6_.refs_7_.refs_8_.refs_9_.refs_2_.refs_3_.rows_ref = bf16[2048,2048]{1,0:T(8,128)(2,1)} custom-call(bf16[512,2048]{1,0:T(8,128)(2,1)} %refs_0_.2, bf16[512,2048]{1,0:T(8,128)(2,1)} %collective-permute-done.4.refs_1_, bf16[512,2048]{1,0:T(8,128)(2,1)} %collective-permute-done.5.refs_2_, ...), custom_call_target="tpu_custom_call" | custom-call | tf_op jit(solution)/shard_map/pallas_call | solution.py:98
  69.8 37.3 %all-gather.3.cloned.1.call-done = bf16[2048,256]{1,0:T(8,128)(2,1)} async-done(((bf16[256,256]{1,0:T(8,128)(2,1)}), bf16[2048,256]{1,0:T(8,128)(2,1)}) %all-gather.3.cloned.1.call-update) | async-done | bytes 1048592 | tf_op jit(solution)/shard_map/all_gather | solution.py:142
  107.1 1.3 constant_dynamic-slice_fusion.3
  108.4 8.8 %convolution_convert_fusion.3 = bf16[256,1024]{1,0:T(8,128)(2,1)} fusion(bf16[2048,1024]{1,0:T(8,128)(2,1)} %param.8, bf16[2048,2048]{1,0:T(8,128)(2,1)} %shard_map.55.refs_5_.refs_6_.refs_7_.refs_8_.refs_9_.refs_2_.refs_3_.rows_ref, bf16[512,256]{1,0:T(8,128)(2,1)S(1)} %get-tuple-element.28, bf16[512,256]{1,0:T(8,128)(2,1)S(1)} %get-tuple-element.29, ...), kind=kOutput, calls=%fused_computation.3 | convolution fusion | flops 3226206208 | bytes 14155776 | tf_op jit(solution)/shard_map/dot_general | solution.py:158
  117.2 2.1 collective-permute-done.1.refs_3_
  119.3 3.2 %collective-permute-start.7 = (bf16[256,4096]{1,0:T(8,128)(2,1)}, bf16[256,4096]{1,0:T(8,128)(2,1)S(1)}, u32[]{:S(2)}, u32[]{:S(2)}) collective-permute-start(bf16[256,4096]{1,0:T(8,128)(2,1)} %collective-permute-done.1.refs_3_), channel_id=1, source_target_pairs={{1,3},{3,5},{5,7},{7,6},{6,4},{4,2},{2,0},{0,1},{9,11},{11,13},{13... | collective-permute-start | bytes 6291464 | tf_op jit(solution)/shard_map/ppermute | solution.py:119
  122.4 1.3 fusion.9.offsets_ref
  123.8 29.6 %shard_map.56.refs_4_ = f32[4096,2048]{1,0:T(8,128)} custom-call(s32[8]{0:T(128)} %fusion.9.offsets_ref, bf16[256,4096]{1,0:T(8,128)(2,1)} %refs_0_.3, bf16[256,4096]{1,0:T(8,128)(2,1)} %copy-done.2, bf16[256,4096]{1,0:T(8,128)(2,1)} %collective-permute-done.2.refs_2_, bf16[256,4096]{1,0:T(8,128)(2,1)} %collective-permute-done.1.refs_3_, ...), custom_call_target="tpu_custom_call" | custom-call | flops 21474836480 | bytes 49283072 | tf_op jit(solution)/shard_map/pallas_call | solution.py:71
  153.4 21.8 %collective-permute-done.7.refs_0_ = bf16[256,4096]{1,0:T(8,128)(2,1)S(1)} collective-permute-done((bf16[256,4096]{1,0:T(8,128)(2,1)}, bf16[256,4096]{1,0:T(8,128)(2,1)S(1)}, u32[]{:S(2)}, u32[]{:S(2)}) %collective-permute-start.7) | collective-permute-done | bytes 2097184 | tf_op jit(solution)/shard_map/ppermute | solution.py:119
  175.4 1.2 copy-done
  176.6 15.0 %shard_map.57.refs_4_ = f32[4096,2048]{1,0:T(8,128)} custom-call(s32[8]{0:T(128)} %fusion.9.offsets_ref, bf16[256,4096]{1,0:T(8,128)(2,1)} %copy-done, bf16[256,4096]{1,0:T(8,128)(2,1)} %collective-permute-done.8.refs_1_, ...), custom_call_target="tpu_custom_call", output_to_operand_aliasing={{}: (5, {})} | custom-call | flops 4294967296 | bytes 37748736 | tf_op jit(solution)/shard_map/pallas_call | solution.py:71
  191.6 9.3 %all-reduce.2.cloned.1.call-done = bf16[256,1024]{1,0:T(8,128)(2,1)} async-done(((bf16[256,1024]{1,0:T(8,128)(2,1)}), bf16[256,1024]{1,0:T(8,128)(2,1)}) %all-reduce.2.cloned.1.call-update) | async-done | bytes 524304 | tf_op jit(solution)/shard_map/psum | solution.py:159
  201.0 2.3 slice.7
  204.4 1.1 collective-permute-start.9
  205.5 15.4 %shard_map.58.total_ref = f32[4096,2048]{1,0:T(8,128)} custom-call(s32[8]{0:T(128)} %fusion.9.offsets_ref, bf16[256,4096]{1,0:T(8,128)(2,1)} %copy-done, bf16[256,4096]{1,0:T(8,128)(2,1)} %collective-permute-done.8.refs_1_, ...), custom_call_target="tpu_custom_call", output_to_operand_aliasing={{}: (5, {})} | custom-call | flops 4294967296 | bytes 37748736 | tf_op jit(solution)/shard_map/pallas_call | solution.py:71
  220.9 3.4 %all-gather.5.cloned.1.call-done = bf16[1024,1024]{1,0:T(8,128)(2,1)} async-done(((bf16[256,1024]{1,0:T(8,128)(2,1)}), bf16[1024,1024]{1,0:T(8,128)(2,1)}) %all-gather.5.cloned.1.call-update) | async-done | bytes 2097168 | tf_op jit(solution)/shard_map/all_gather | solution.py:178
  224.3 9.3 %convolution_convert_fusion.factor_ref = bf16[1024,2048]{1,0:T(8,128)(2,1)} fusion(bf16[1024,1024]{1,0:T(8,128)(2,1)} %all-gather.5.cloned.1.call-done, bf16[2048,1024]{1,0:T(8,128)(2,1)} %param.8), kind=kOutput, calls=%fused_computation | convolution fusion | flops 4297064448 | bytes 10485760 | tf_op jit(solution)/shard_map/dot_general | solution.py:183
  235.6 36.0 %shard_map.59 = f32[4096,2048]{1,0:T(8,128)} custom-call(s32[8]{0:T(128)} %fusion.9.offsets_ref, bf16[256,2048]{1,0:T(8,128)(2,1)} %copy-done.4, bf16[256,2048]{1,0:T(8,128)(2,1)} %copy-done.3, bf16[2048,2048]{1,0:T(8,128)(2,1)} %shard_map.55.refs_5_.refs_6_.refs_7_.refs_8_.refs_9_.refs_2_.refs_3_.rows_ref, ...), custom_call_target="tpu_custom_call", output_to_operand_aliasing={{}: (6, {})} | custom-call | tf_op jit(solution)/shard_map/pallas_call | solution.py:203
  (32 shorter events, 4.4 us)
Async XLA Ops:
  6.5 51.7 %reduce-scatter.2.cloned.1.call-start = ((), (), s32[]{:S(2)}) async-start(), calls=%async_computation.1 | async-start | bytes 655360 | tf_op jit(solution)/shard_map/reduce_scatter | solution.py:138
  6.5 51.7 %collective-permute-start.5 = (bf16[512,2048]{1,0:T(8,128)(2,1)}, bf16[512,2048]{1,0:T(8,128)(2,1)}, u32[]{:S(2)}, u32[]{:S(2)}) collective-permute-start(bf16[512,2048]{1,0:T(8,128)(2,1)} %refs_0_.2), channel_id=1, source_target_pairs={{0,16},{8,24},{16,0},{24,8},{1,17},{9,25},{17,1},{25,9},{2,18},{10... | collective-permute-start | bytes 6291464 | tf_op jit(solution)/shard_map/ppermute | solution.py:148
  9.5 48.8 %collective-permute-start = (bf16[256,4096]{1,0:T(8,128)(2,1)}, bf16[256,4096]{1,0:T(8,128)(2,1)S(1)}, u32[]{:S(2)}, u32[]{:S(2)}) collective-permute-start(bf16[256,4096]{1,0:T(8,128)(2,1)} %refs_0_.3), channel_id=1, source_target_pairs={{1,3},{3,5},{5,7},{7,6},{6,4},{4,2},{2,0},{0,1},{9,11},{11,13},{13... | collective-permute-start | bytes 6291464 | tf_op jit(solution)/shard_map/ppermute | solution.py:119
  11.0 49.2 %collective-permute-start.2 = (bf16[256,4096]{1,0:T(8,128)(2,1)}, bf16[256,4096]{1,0:T(8,128)(2,1)}, u32[]{:S(2)}, u32[]{:S(2)}) collective-permute-start(bf16[256,4096]{1,0:T(8,128)(2,1)} %refs_0_.3), channel_id=1, source_target_pairs={{3,1},{5,3},{7,5},{6,7},{4,6},{2,4},{0,2},{1,0},{11,9},{13,11},{15... | collective-permute-start | bytes 6291464 | tf_op jit(solution)/shard_map/ppermute | solution.py:122
  18.7 88.5 %all-gather.3.cloned.1.call-start = ((), (), s32[]{:S(2)}) async-start(), calls=%async_computation.2 | async-start | bytes 1179648 | tf_op jit(solution)/shard_map/all_gather | solution.py:142
  18.7 41.7 %collective-permute-start.4 = (bf16[512,2048]{1,0:T(8,128)(2,1)}, bf16[512,2048]{1,0:T(8,128)(2,1)}, u32[]{:S(2)}, u32[]{:S(2)}) collective-permute-start(bf16[512,2048]{1,0:T(8,128)(2,1)} %refs_0_.2), channel_id=1, source_target_pairs={{0,8},{8,0},{16,24},{24,16},{1,9},{9,1},{17,25},{25,17},{2,10},{10... | collective-permute-start | bytes 6291464 | tf_op jit(solution)/shard_map/ppermute | solution.py:148
  58.2 4.5 %collective-permute-start.6 = (bf16[512,2048]{1,0:T(8,128)(2,1)}, bf16[512,2048]{1,0:T(8,128)(2,1)}, u32[]{:S(2)}, u32[]{:S(2)}) collective-permute-start(bf16[512,2048]{1,0:T(8,128)(2,1)} %collective-permute-done.5.refs_2_), channel_id=1, source_target_pairs={{0,8},{8,0},{16,24},{24,16},{1,9},{9,1},{17,25},{25,17},{2,10},{10... | collective-permute-start | bytes 6291464 | tf_op jit(solution)/shard_map/ppermute | solution.py:148
  58.3 142.7 %all-reduce.2.cloned.1.call-start = ((), (), s32[]{:S(2)}) async-start(), calls=%async_computation.3 | async-start | bytes 1048576 | tf_op jit(solution)/shard_map/psum | solution.py:159
  58.3 11.5 %copy-start.2 = (bf16[256,4096]{1,0:T(8,128)(2,1)}, bf16[256,4096]{1,0:T(8,128)(2,1)S(1)}, u32[]{:S(2)}) copy-start(bf16[256,4096]{1,0:T(8,128)(2,1)S(1)} %collective-permute-done.refs_1_) | copy-start | bytes 6291460
  58.3 60.9 %collective-permute-start.1 = (bf16[256,4096]{1,0:T(8,128)(2,1)S(1)}, bf16[256,4096]{1,0:T(8,128)(2,1)}, u32[]{:S(2)}, u32[]{:S(2)}) collective-permute-start(bf16[256,4096]{1,0:T(8,128)(2,1)S(1)} %collective-permute-done.refs_1_), channel_id=1, source_target_pairs={{1,3},{3,5},{5,7},{7,6},{6,4},{4,2},{2,0},{0,1},{9,11},{11,13},{13... | collective-permute-start | bytes 6291464 | tf_op jit(solution)/shard_map/ppermute | solution.py:119
  60.2 59.1 %collective-permute-start.3 = (bf16[256,4096]{1,0:T(8,128)(2,1)}, bf16[256,4096]{1,0:T(8,128)(2,1)}, u32[]{:S(2)}, u32[]{:S(2)}) collective-permute-start(bf16[256,4096]{1,0:T(8,128)(2,1)} %collective-permute-done.2.refs_2_), channel_id=1, source_target_pairs={{3,1},{5,3},{7,5},{6,7},{4,6},{2,4},{0,2},{1,0},{11,9},{13,11},{15... | collective-permute-start | bytes 6291464 | tf_op jit(solution)/shard_map/ppermute | solution.py:122
  119.3 55.9 %collective-permute-start.7 = (bf16[256,4096]{1,0:T(8,128)(2,1)}, bf16[256,4096]{1,0:T(8,128)(2,1)S(1)}, u32[]{:S(2)}, u32[]{:S(2)}) collective-permute-start(bf16[256,4096]{1,0:T(8,128)(2,1)} %collective-permute-done.1.refs_3_), channel_id=1, source_target_pairs={{1,3},{3,5},{5,7},{7,6},{6,4},{4,2},{2,0},{0,1},{9,11},{11,13},{13... | collective-permute-start | bytes 6291464 | tf_op jit(solution)/shard_map/ppermute | solution.py:119
  122.4 52.9 %collective-permute-start.8 = (bf16[256,4096]{1,0:T(8,128)(2,1)}, bf16[256,4096]{1,0:T(8,128)(2,1)}, u32[]{:S(2)}, u32[]{:S(2)}) collective-permute-start(bf16[256,4096]{1,0:T(8,128)(2,1)} %collective-permute-done.3.refs_4_), channel_id=1, source_target_pairs={{3,1},{5,3},{7,5},{6,7},{4,6},{2,4},{0,2},{1,0},{11,9},{13,11},{15... | collective-permute-start | bytes 6291464 | tf_op jit(solution)/shard_map/ppermute | solution.py:122
  123.7 100.5 %all-gather.5.cloned.1.call-start = ((), (), s32[]{:S(2)}) async-start(), calls=%async_computation.4 | async-start | bytes 2621440 | tf_op jit(solution)/shard_map/all_gather | solution.py:178
  175.2 1.4 copy-start
  191.6 11.7 %copy-start.1 = (bf16[256,4096]{1,0:T(8,128)(2,1)S(1)}, bf16[256,4096]{1,0:T(8,128)(2,1)}, u32[]{:S(2)}) copy-start(bf16[256,4096]{1,0:T(8,128)(2,1)} %copy-done) | copy-start | bytes 6291460
  203.4 30.2 %collective-permute-start.10 = (bf16[256,2048]{1,0:T(8,128)(2,1)}, bf16[256,2048]{1,0:T(8,128)(2,1)S(1)}, u32[]{:S(2)}, u32[]{:S(2)}) collective-permute-start(bf16[256,2048]{1,0:T(8,128)(2,1)} %slice.7), channel_id=1, source_target_pairs={{3,1},{5,3},{7,5},{6,7},{4,6},{2,4},{0,2},{1,0},{11,9},{13,11},{15... | collective-permute-start | bytes 3145736 | tf_op jit(solution)/shard_map/ppermute | solution.py:122
  204.4 29.2 %collective-permute-start.9 = (bf16[256,2048]{1,0:T(8,128)(2,1)S(1)}, bf16[256,2048]{1,0:T(8,128)(2,1)S(1)}, u32[]{:S(2)}, u32[]{:S(2)}) collective-permute-start(bf16[256,2048]{1,0:T(8,128)(2,1)S(1)} %slice.6), channel_id=1, source_target_pairs={{1,3},{3,5},{5,7},{7,6},{6,4},{4,2},{2,0},{0,1},{9,11},{11,13},{13... | collective-permute-start | bytes 3145736 | tf_op jit(solution)/shard_map/ppermute | solution.py:119
  233.6 1.0 copy-start.3
  234.6 1.0 copy-start.4
Sparse Core Ops, SparseCore 0:
  18.8 24.8 reduce-scatter.1
  58.4 48.6 all-gather.2
  123.9 77.0 all-reduce.1
  202.4 21.8 all-gather.4

commit v3 on v2

--- a/solution.py
+++ b/solution.py
@@ -149,7 +149,7 @@
         bit //= 2
     rows = stacked([slots[k] for k in range(outs)])
 
-    coefficients = after(coefficients, ups, downs, rows)
+    coefficients = after(coefficients, ups, downs, rows, offsets)
     block = coefficients.shape[0] // outs
     coefficients = jnp.concatenate(
         [lax.dynamic_slice_in_dim(coefficients, (mine ^ k) * block, block, axis=0) for k in range(outs)], axis=0

time: 278 us -> 277 us (level)
  no operation moved by 1% of the time
where the time goes in v3:
time: 277 us
  waiting for transfers between devices  115 us (42%)
  Pallas kernels  103 us (37%)
  matrix products  25.3 us (9%)
  between operations  13.2 us (5%)
  starting transfers between devices  12.5 us (5%)
  local copies, waits for them, and re-layouts  8.17 us (3%)
    pallas_call x3, Pallas kernels, add_products(): pl.pallas_call(kernel, out_shape=jax.ShapeDtypeStruct((height, width), lo...  60 us
    ppermute x3, waiting for transfers between devices, body(): lax.ppermute(v, 'out', swap)  40.5 us
    all_gather x1, waiting for transfers between devices, body(): coefficients = lax.all_gather(share, 'in', axis=0, tiled=True)  37.3 us
    pallas_call x1, Pallas kernels, remove(): pl.pallas_call(kernel, out_shape=jax.ShapeDtypeStruct((height, width), F3...  36 us
    ppermute x4, waiting for transfers between devices, up(): return lax.ppermute(x, 'in', forward)  25.4 us
    dot_general x1, matrix products, body(): factor = jnp.dot(core, basis_in.T, preferred_element_type=F32).astype(BF16)  9.33 us
    dot_general x1, matrix products, body(): core_part = jnp.dot(seen, basis_in, preferred_element_type=F32).astype(BF16)  8.8 us
    psum x1, waiting for transfers between devices, body(): core = lax.psum(core_part, 'in')  7.88 us
  transfers between devices with their start and end apart: 15, of which 8 were waited for; matrix products, arithmetic and copies ran while one was open for 11% of the time, Pallas kernels for 24%

profile of v3, /device:TPU:0, one launch (start us, length us, event | category | flops | bytes accessed | tf_op | source)
XLA Modules:
  0.0 276.9 jit_solution(8276186694093005838)
XLA Ops:
  6.5 2.9 %collective-permute-start.5 = (bf16[512,2048]{1,0:T(8,128)(2,1)}, bf16[512,2048]{1,0:T(8,128)(2,1)}, u32[]{:S(2)}, u32[]{:S(2)}) collective-permute-start(bf16[512,2048]{1,0:T(8,128)(2,1)} %refs_0_.2), channel_id=1, source_target_pairs={{0,16},{8,24},{16,0},{24,8},{1,17},{9,25},{17,1},{25,9},{2,18},{10... | collective-permute-start | bytes 6291464 | tf_op jit(solution)/shard_map/ppermute | solution.py:148
  9.5 1.5 collective-permute-start
  11.5 7.1 %convolution_convert_fusion.2 = bf16[256,1024]{1,0:T(8,128)(2,1)} fusion(bf16[256,4096]{1,0:T(8,128)(2,1)} %refs_0_.3, bf16[4096,1024]{1,0:T(8,128)(2,1)} %basis_ref.1), kind=kOutput, calls=%fused_computation.2 | convolution fusion | flops 2147745792 | bytes 11010048 | tf_op jit(solution)/shard_map/dot_general | solution.py:139
  18.8 39.4 %collective-permute-done.5.refs_2_ = bf16[512,2048]{1,0:T(8,128)(2,1)} collective-permute-done((bf16[512,2048]{1,0:T(8,128)(2,1)}, bf16[512,2048]{1,0:T(8,128)(2,1)}, u32[]{:S(2)}, u32[]{:S(2)}) %collective-permute-start.5) | collective-permute-done | bytes 2097184 | tf_op jit(solution)/shard_map/ppermute | solution.py:148
  58.3 1.8 collective-permute-start.1
  60.4 1.2 fusion.9.offsets_ref
  61.7 1.1 collective-permute-done.6.refs_3_
  62.7 7.1 %shard_map.55.refs_5_.refs_6_.refs_7_.refs_8_.refs_9_.refs_2_.refs_3_.rows_ref = bf16[2048,2048]{1,0:T(8,128)(2,1)} custom-call(bf16[512,2048]{1,0:T(8,128)(2,1)} %refs_0_.2, bf16[512,2048]{1,0:T(8,128)(2,1)} %collective-permute-done.4.refs_1_, bf16[512,2048]{1,0:T(8,128)(2,1)} %collective-permute-done.5.refs_2_, ...), custom_call_target="tpu_custom_call" | custom-call | tf_op jit(solution)/shard_map/pallas_call | solution.py:98
  69.8 37.3 %all-gather.3.cloned.1.call-done = bf16[2048,256]{1,0:T(8,128)(2,1)} async-done(((bf16[256,256]{1,0:T(8,128)(2,1)}), bf16[2048,256]{1,0:T(8,128)(2,1)}) %all-gather.3.cloned.1.call-update) | async-done | bytes 1048592 | tf_op jit(solution)/shard_map/all_gather | solution.py:142
  107.1 1.3 constant_dynamic-slice_fusion.3
  108.4 8.8 %convolution_convert_fusion.3 = bf16[256,1024]{1,0:T(8,128)(2,1)} fusion(bf16[2048,1024]{1,0:T(8,128)(2,1)} %param.8, bf16[2048,2048]{1,0:T(8,128)(2,1)} %shard_map.55.refs_5_.refs_6_.refs_7_.refs_8_.refs_9_.refs_2_.refs_3_.rows_ref, bf16[512,256]{1,0:T(8,128)(2,1)S(1)} %get-tuple-element.28, bf16[512,256]{1,0:T(8,128)(2,1)S(1)} %get-tuple-element.29, ...), kind=kOutput, calls=%fused_computation.3 | convolution fusion | flops 3226206208 | bytes 14155776 | tf_op jit(solution)/shard_map/dot_general | solution.py:158
  117.2 2.1 collective-permute-done.1.refs_3_
  119.3 3.2 %collective-permute-start.7 = (bf16[256,4096]{1,0:T(8,128)(2,1)}, bf16[256,4096]{1,0:T(8,128)(2,1)S(1)}, u32[]{:S(2)}, u32[]{:S(2)}) collective-permute-start(bf16[256,4096]{1,0:T(8,128)(2,1)} %collective-permute-done.1.refs_3_), channel_id=1, source_target_pairs={{1,3},{3,5},{5,7},{7,6},{6,4},{4,2},{2,0},{0,1},{9,11},{11,13},{13... | collective-permute-start | bytes 6291464 | tf_op jit(solution)/shard_map/ppermute | solution.py:119
  122.5 29.6 %shard_map.56.refs_4_ = f32[4096,2048]{1,0:T(8,128)} custom-call(s32[8]{0:T(128)} %fusion.9.offsets_ref, bf16[256,4096]{1,0:T(8,128)(2,1)} %refs_0_.3, bf16[256,4096]{1,0:T(8,128)(2,1)} %copy-done.2, bf16[256,4096]{1,0:T(8,128)(2,1)} %collective-permute-done.2.refs_2_, bf16[256,4096]{1,0:T(8,128)(2,1)} %collective-permute-done.1.refs_3_, ...), custom_call_target="tpu_custom_call" | custom-call | flops 21474836480 | bytes 49283072 | tf_op jit(solution)/shard_map/pallas_call | solution.py:71
  152.1 23.3 %collective-permute-done.7.refs_0_ = bf16[256,4096]{1,0:T(8,128)(2,1)S(1)} collective-permute-done((bf16[256,4096]{1,0:T(8,128)(2,1)}, bf16[256,4096]{1,0:T(8,128)(2,1)S(1)}, u32[]{:S(2)}, u32[]{:S(2)}) %collective-permute-start.7) | collective-permute-done | bytes 2097184 | tf_op jit(solution)/shard_map/ppermute | solution.py:119
  175.6 1.3 copy-done
  176.8 15.1 %shard_map.57.refs_4_ = f32[4096,2048]{1,0:T(8,128)} custom-call(s32[8]{0:T(128)} %fusion.9.offsets_ref, bf16[256,4096]{1,0:T(8,128)(2,1)} %copy-done, bf16[256,4096]{1,0:T(8,128)(2,1)} %collective-permute-done.8.refs_1_, ...), custom_call_target="tpu_custom_call", output_to_operand_aliasing={{}: (5, {})} | custom-call | flops 4294967296 | bytes 37748736 | tf_op jit(solution)/shard_map/pallas_call | solution.py:71
  191.9 7.9 %all-reduce.2.cloned.1.call-done = bf16[256,1024]{1,0:T(8,128)(2,1)} async-done(((bf16[256,1024]{1,0:T(8,128)(2,1)}), bf16[256,1024]{1,0:T(8,128)(2,1)}) %all-reduce.2.cloned.1.call-update) | async-done | bytes 524304 | tf_op jit(solution)/shard_map/psum | solution.py:159
  199.8 2.3 slice.7
  203.2 1.1 collective-permute-start.9
  204.3 15.4 %shard_map.58.total_ref = f32[4096,2048]{1,0:T(8,128)} custom-call(s32[8]{0:T(128)} %fusion.9.offsets_ref, bf16[256,4096]{1,0:T(8,128)(2,1)} %copy-done, bf16[256,4096]{1,0:T(8,128)(2,1)} %collective-permute-done.8.refs_1_, ...), custom_call_target="tpu_custom_call", output_to_operand_aliasing={{}: (5, {})} | custom-call | flops 4294967296 | bytes 37748736 | tf_op jit(solution)/shard_map/pallas_call | solution.py:71
  219.7 3.4 %all-gather.5.cloned.1.call-done = bf16[1024,1024]{1,0:T(8,128)(2,1)} async-done(((bf16[256,1024]{1,0:T(8,128)(2,1)}), bf16[1024,1024]{1,0:T(8,128)(2,1)}) %all-gather.5.cloned.1.call-update) | async-done | bytes 2097168 | tf_op jit(solution)/shard_map/all_gather | solution.py:178
  223.1 9.3 %convolution_convert_fusion.factor_ref = bf16[1024,2048]{1,0:T(8,128)(2,1)} fusion(bf16[1024,1024]{1,0:T(8,128)(2,1)} %all-gather.5.cloned.1.call-done, bf16[2048,1024]{1,0:T(8,128)(2,1)} %param.8), kind=kOutput, calls=%fused_computation | convolution fusion | flops 4297064448 | bytes 10485760 | tf_op jit(solution)/shard_map/dot_general | solution.py:183
  234.4 36.0 %shard_map.59 = f32[4096,2048]{1,0:T(8,128)} custom-call(s32[8]{0:T(128)} %fusion.9.offsets_ref, bf16[256,2048]{1,0:T(8,128)(2,1)} %copy-done.4, bf16[256,2048]{1,0:T(8,128)(2,1)} %copy-done.3, bf16[2048,2048]{1,0:T(8,128)(2,1)} %shard_map.55.refs_5_.refs_6_.refs_7_.refs_8_.refs_9_.refs_2_.refs_3_.rows_ref, ...), custom_call_target="tpu_custom_call", output_to_operand_aliasing={{}: (6, {})} | custom-call | tf_op jit(solution)/shard_map/pallas_call | solution.py:203
  (32 shorter events, 4.3 us)
Async XLA Ops:
  6.5 51.7 %reduce-scatter.2.cloned.1.call-start = ((), (), s32[]{:S(2)}) async-start(), calls=%async_computation.1 | async-start | bytes 655360 | tf_op jit(solution)/shard_map/reduce_scatter | solution.py:138
  6.5 51.7 %collective-permute-start.5 = (bf16[512,2048]{1,0:T(8,128)(2,1)}, bf16[512,2048]{1,0:T(8,128)(2,1)}, u32[]{:S(2)}, u32[]{:S(2)}) collective-permute-start(bf16[512,2048]{1,0:T(8,128)(2,1)} %refs_0_.2), channel_id=1, source_target_pairs={{0,16},{8,24},{16,0},{24,8},{1,17},{9,25},{17,1},{25,9},{2,18},{10... | collective-permute-start | bytes 6291464 | tf_op jit(solution)/shard_map/ppermute | solution.py:148
  9.5 48.8 %collective-permute-start = (bf16[256,4096]{1,0:T(8,128)(2,1)}, bf16[256,4096]{1,0:T(8,128)(2,1)S(1)}, u32[]{:S(2)}, u32[]{:S(2)}) collective-permute-start(bf16[256,4096]{1,0:T(8,128)(2,1)} %refs_0_.3), channel_id=1, source_target_pairs={{1,3},{3,5},{5,7},{7,6},{6,4},{4,2},{2,0},{0,1},{9,11},{11,13},{13... | collective-permute-start | bytes 6291464 | tf_op jit(solution)/shard_map/ppermute | solution.py:119
  11.0 49.2 %collective-permute-start.2 = (bf16[256,4096]{1,0:T(8,128)(2,1)}, bf16[256,4096]{1,0:T(8,128)(2,1)}, u32[]{:S(2)}, u32[]{:S(2)}) collective-permute-start(bf16[256,4096]{1,0:T(8,128)(2,1)} %refs_0_.3), channel_id=1, source_target_pairs={{3,1},{5,3},{7,5},{6,7},{4,6},{2,4},{0,2},{1,0},{11,9},{13,11},{15... | collective-permute-start | bytes 6291464 | tf_op jit(solution)/shard_map/ppermute | solution.py:122
  18.7 88.5 %all-gather.3.cloned.1.call-start = ((), (), s32[]{:S(2)}) async-start(), calls=%async_computation.2 | async-start | bytes 1179648 | tf_op jit(solution)/shard_map/all_gather | solution.py:142
  18.7 42.9 %collective-permute-start.4 = (bf16[512,2048]{1,0:T(8,128)(2,1)}, bf16[512,2048]{1,0:T(8,128)(2,1)}, u32[]{:S(2)}, u32[]{:S(2)}) collective-permute-start(bf16[512,2048]{1,0:T(8,128)(2,1)} %refs_0_.2), channel_id=1, source_target_pairs={{0,8},{8,0},{16,24},{24,16},{1,9},{9,1},{17,25},{25,17},{2,10},{10... | collective-permute-start | bytes 6291464 | tf_op jit(solution)/shard_map/ppermute | solution.py:148
  58.2 4.5 %collective-permute-start.6 = (bf16[512,2048]{1,0:T(8,128)(2,1)}, bf16[512,2048]{1,0:T(8,128)(2,1)}, u32[]{:S(2)}, u32[]{:S(2)}) collective-permute-start(bf16[512,2048]{1,0:T(8,128)(2,1)} %collective-permute-done.5.refs_2_), channel_id=1, source_target_pairs={{0,8},{8,0},{16,24},{24,16},{1,9},{9,1},{17,25},{25,17},{2,10},{10... | collective-permute-start | bytes 6291464 | tf_op jit(solution)/shard_map/ppermute | solution.py:148
  58.3 141.5 %all-reduce.2.cloned.1.call-start = ((), (), s32[]{:S(2)}) async-start(), calls=%async_computation.3 | async-start | bytes 1048576 | tf_op jit(solution)/shard_map/psum | solution.py:159
  58.3 11.5 %copy-start.2 = (bf16[256,4096]{1,0:T(8,128)(2,1)}, bf16[256,4096]{1,0:T(8,128)(2,1)S(1)}, u32[]{:S(2)}) copy-start(bf16[256,4096]{1,0:T(8,128)(2,1)S(1)} %collective-permute-done.refs_1_) | copy-start | bytes 6291460
  58.3 60.9 %collective-permute-start.1 = (bf16[256,4096]{1,0:T(8,128)(2,1)S(1)}, bf16[256,4096]{1,0:T(8,128)(2,1)}, u32[]{:S(2)}, u32[]{:S(2)}) collective-permute-start(bf16[256,4096]{1,0:T(8,128)(2,1)S(1)} %collective-permute-done.refs_1_), channel_id=1, source_target_pairs={{1,3},{3,5},{5,7},{7,6},{6,4},{4,2},{2,0},{0,1},{9,11},{11,13},{13... | collective-permute-start | bytes 6291464 | tf_op jit(solution)/shard_map/ppermute | solution.py:119
  60.2 59.1 %collective-permute-start.3 = (bf16[256,4096]{1,0:T(8,128)(2,1)}, bf16[256,4096]{1,0:T(8,128)(2,1)}, u32[]{:S(2)}, u32[]{:S(2)}) collective-permute-start(bf16[256,4096]{1,0:T(8,128)(2,1)} %collective-permute-done.2.refs_2_), channel_id=1, source_target_pairs={{3,1},{5,3},{7,5},{6,7},{4,6},{2,4},{0,2},{1,0},{11,9},{13,11},{15... | collective-permute-start | bytes 6291464 | tf_op jit(solution)/shard_map/ppermute | solution.py:122
  119.3 56.2 %collective-permute-start.7 = (bf16[256,4096]{1,0:T(8,128)(2,1)}, bf16[256,4096]{1,0:T(8,128)(2,1)S(1)}, u32[]{:S(2)}, u32[]{:S(2)}) collective-permute-start(bf16[256,4096]{1,0:T(8,128)(2,1)} %collective-permute-done.1.refs_3_), channel_id=1, source_target_pairs={{1,3},{3,5},{5,7},{7,6},{6,4},{4,2},{2,0},{0,1},{9,11},{11,13},{13... | collective-permute-start | bytes 6291464 | tf_op jit(solution)/shard_map/ppermute | solution.py:119
  122.4 53.1 %collective-permute-start.8 = (bf16[256,4096]{1,0:T(8,128)(2,1)}, bf16[256,4096]{1,0:T(8,128)(2,1)}, u32[]{:S(2)}, u32[]{:S(2)}) collective-permute-start(bf16[256,4096]{1,0:T(8,128)(2,1)} %collective-permute-done.3.refs_4_), channel_id=1, source_target_pairs={{3,1},{5,3},{7,5},{6,7},{4,6},{2,4},{0,2},{1,0},{11,9},{13,11},{15... | collective-permute-start | bytes 6291464 | tf_op jit(solution)/shard_map/ppermute | solution.py:122
  122.5 100.6 %all-gather.5.cloned.1.call-start = ((), (), s32[]{:S(2)}) async-start(), calls=%async_computation.4 | async-start | bytes 2621440 | tf_op jit(solution)/shard_map/all_gather | solution.py:178
  175.4 1.4 copy-start
  191.9 10.2 %copy-start.1 = (bf16[256,4096]{1,0:T(8,128)(2,1)S(1)}, bf16[256,4096]{1,0:T(8,128)(2,1)}, u32[]{:S(2)}) copy-start(bf16[256,4096]{1,0:T(8,128)(2,1)} %copy-done) | copy-start | bytes 6291460
  202.2 30.2 %collective-permute-start.10 = (bf16[256,2048]{1,0:T(8,128)(2,1)}, bf16[256,2048]{1,0:T(8,128)(2,1)S(1)}, u32[]{:S(2)}, u32[]{:S(2)}) collective-permute-start(bf16[256,2048]{1,0:T(8,128)(2,1)} %slice.7), channel_id=1, source_target_pairs={{3,1},{5,3},{7,5},{6,7},{4,6},{2,4},{0,2},{1,0},{11,9},{13,11},{15... | collective-permute-start | bytes 3145736 | tf_op jit(solution)/shard_map/ppermute | solution.py:122
  203.2 29.2 %collective-permute-start.9 = (bf16[256,2048]{1,0:T(8,128)(2,1)S(1)}, bf16[256,2048]{1,0:T(8,128)(2,1)S(1)}, u32[]{:S(2)}, u32[]{:S(2)}) collective-permute-start(bf16[256,2048]{1,0:T(8,128)(2,1)S(1)} %slice.6), channel_id=1, source_target_pairs={{1,3},{3,5},{5,7},{7,6},{6,4},{4,2},{2,0},{0,1},{9,11},{11,13},{13... | collective-permute-start | bytes 3145736 | tf_op jit(solution)/shard_map/ppermute | solution.py:119
  232.4 1.0 copy-start.3
  233.4 1.0 copy-start.4
Sparse Core Ops, SparseCore 0:
  18.8 24.8 reduce-scatter.1
  58.4 48.6 all-gather.2
  122.6 77.1 all-reduce.1
  201.2 21.8 all-gather.4
